TPU v7x, 32 devices: a whole 2x2x4 slice. The times are simulated.
32 devices in a mesh: dp: 16 (over z, y, x), tp: 2 (over core).
Axes of the slice: x: 2, y: 2, z: 4, core: 2. Of those that a mesh axis runs over, the one named last changes fastest.
Arguments:
- tokens: bfloat16 [25216, 1024], P(('dp', 'tp')), may hold values from -6 to 6
- masked: int32 [25216], P(('dp', 'tp')), may hold values from 0 to 1, as said below
- cotangent: bfloat16 [25216, 1024], P(('dp', 'tp')), may hold values from -6 to 6
- mask_token: float32 [1024], replicated, may hold values from -6 to 6
- gain_one: float32 [1024], replicated, may hold values from 0.5 to 1.5
- shift_one: float32 [1024], replicated, may hold values from -2 to 2
- w_query: bfloat16 [1024, 1024], P(None, 'tp'), may hold values from -0.1875 to 0.1875
- w_key: bfloat16 [1024, 1024], P(None, 'tp'), may hold values from -0.1875 to 0.1875
- w_value: bfloat16 [1024, 1024], P(None, 'tp'), may hold values from -0.1875 to 0.1875
- b_query: float32 [1024], P('tp'), may hold values from -3 to 3
- b_value: float32 [1024], P('tp'), may hold values from -3 to 3
- w_out: bfloat16 [1024, 1024], P('tp'), may hold values from -1 to 1
- b_out: float32 [1024], replicated, may hold values from -3 to 3
- scale_one: float32 [1024], replicated, may hold values from 0.5 to 1.5
- gain_two: float32 [1024], replicated, may hold values from 0.5 to 1.5
- shift_two: float32 [1024], replicated, may hold values from -2 to 2
- w_up: bfloat16 [1024, 4096], P(None, 'tp'), may hold values from -0.1875 to 0.1875
- b_up: float32 [4096], P('tp'), may hold values from -3 to 3
- w_down: bfloat16 [4096, 1024], P('tp'), may hold values from -0.125 to 0.125
- b_down: float32 [1024], replicated, may hold values from -3 to 3
- scale_two: float32 [1024], replicated, may hold values from 0.5 to 1.5
Outputs:
- block_out: bfloat16 [25216, 1024], P(('dp', 'tp'))
- grad_tokens: float32 [25216, 1024], P(('dp', 'tp'))
- grad_mask_token: float32 [1024], replicated
- grad_gain_one: float32 [1024], replicated
- grad_shift_one: float32 [1024], replicated
- grad_w_query: float32 [1024, 1024], P('dp', 'tp')
- grad_w_key: float32 [1024, 1024], P('dp', 'tp')
- grad_w_value: float32 [1024, 1024], P('dp', 'tp')
- grad_b_query: float32 [1024], P('tp')
- grad_b_value: float32 [1024], P('tp')
- grad_w_out: float32 [1024, 1024], P('tp', 'dp')
- grad_b_out: float32 [1024], replicated
- grad_scale_one: float32 [1024], replicated
- grad_gain_two: float32 [1024], replicated
- grad_shift_two: float32 [1024], replicated
- grad_w_up: float32 [1024, 4096], P('dp', 'tp')
- grad_b_up: float32 [4096], P('tp')
- grad_w_down: float32 [4096, 1024], P('tp', 'dp')
- grad_b_down: float32 [1024], replicated
- grad_scale_two: float32 [1024], replicated
Inputs may be any that keep to these rules, and one draw needn't show every extreme that they name: `masked`: in each image of 197 rows the first (class) row is 0; of the other rows, between two fifths (rounded up) and four fifths (rounded down) are 1, a number that varies from image to image.
All inputs are finite; a program needn't handle non-finite values.
Results may differ from a plain program's by a relative error of at most 0.023.
Values may be sent and summed in bfloat16 or wider, within the bound.
No kernel may reach another device: no remote copies, remote signals or barrier semaphores. Data moves between devices by JAX's collectives and lax.ppermute only.
A program may use at most 256 MiB of HBM per device.

v0:
```python
import math

import jax
import jax.numpy as jnp
from jax import lax
from jax.sharding import PartitionSpec as P

SEQ = 197
HD = 64


EPSILON = 1e-06


def layer_norm(rows_in, gain_vec, shift_vec):
    center = rows_in - jnp.mean(rows_in, axis=-1, keepdims=True)
    spread = jnp.mean(center * center, axis=-1, keepdims=True)
    return center * lax.rsqrt(spread + EPSILON) * gain_vec + shift_vec


def norm_backward(rows_in, gain_vec, shift_vec, grad_rows):
    unused, pull = jax.vjp(layer_norm, rows_in, gain_vec, shift_vec)
    return pull(grad_rows)


def gelu_exact(values):
    return jax.nn.gelu(values, approximate=False)


def product(left, right):
    return jnp.dot(left, right, preferred_element_type=jnp.float32)


def times_transposed(left, right):
    return lax.dot_general(
        left, right, (((1,), (1,)), ((), ())), preferred_element_type=jnp.float32
    )


def transposed_times(left, right):
    return lax.dot_general(
        left, right, (((0,), (0,)), ((), ())), preferred_element_type=jnp.float32
    )


def attend_forward(queries, key_rows, values, factor):
    scores = (
        jnp.einsum("iqhd,ikhd->ihqk", queries, key_rows, preferred_element_type=jnp.float32)
        * factor
    )
    row_max = jnp.max(scores, axis=-1, keepdims=True)
    raised = jnp.exp(scores - row_max)
    sum_exp = jnp.sum(raised, axis=-1, keepdims=True)
    probs_low = (raised / sum_exp).astype(jnp.bfloat16)
    context = jnp.einsum("ihqk,ikhd->iqhd", probs_low, values, preferred_element_type=jnp.float32)
    return (context, row_max + jnp.log(sum_exp))


def attend_backward(queries, key_rows, values, log_total, grad_context, factor):
    scores = (
        jnp.einsum("iqhd,ikhd->ihqk", queries, key_rows, preferred_element_type=jnp.float32)
        * factor
    )
    probs = jnp.exp(scores - log_total)
    grad_probs = jnp.einsum(
        "iqhd,ikhd->ihqk", grad_context, values, preferred_element_type=jnp.float32
    )
    inner = jnp.sum(grad_probs * probs, axis=-1, keepdims=True)
    grad_scores = (probs * (grad_probs - inner)).astype(jnp.bfloat16)
    grad_queries = (
        jnp.einsum("ihqk,ikhd->iqhd", grad_scores, key_rows, preferred_element_type=jnp.float32)
        * factor
    )
    grad_keys = (
        jnp.einsum("ihqk,iqhd->ikhd", grad_scores, queries, preferred_element_type=jnp.float32)
        * factor
    )
    grad_values = jnp.einsum(
        "ihqk,iqhd->ikhd",
        probs.astype(jnp.bfloat16),
        grad_context,
        preferred_element_type=jnp.float32,
    )
    return (grad_queries, grad_keys, grad_values)


def body(
    tokens,
    masked,
    cotangent,
    mask_token,
    gain_one,
    shift_one,
    w_query,
    w_key,
    w_value,
    b_query,
    b_value,
    w_out,
    b_out,
    scale_one,
    gain_two,
    shift_two,
    w_up,
    b_up,
    w_down,
    b_down,
    scale_two,
):
    local_cols = w_query.shape[1]
    local_heads = local_cols // HD
    factor = 1.0 / math.sqrt(HD)
    chosen = (masked > 0)[:, None]
    initial = jnp.where(chosen, mask_token[None, :], tokens.astype(jnp.float32))
    normed = layer_norm(initial, gain_one, shift_one).astype(jnp.bfloat16)
    w_joined = jnp.concatenate([w_query, w_key, w_value], axis=1)
    b_joined = jnp.concatenate([b_query, jnp.zeros_like(b_query), b_value])
    gathered = lax.all_gather(normed, "tp", axis=0, tiled=True)
    joined = (product(gathered, w_joined) + b_joined).astype(jnp.bfloat16)
    group_rows = gathered.shape[0]
    head_shape = (group_rows // SEQ, SEQ, local_heads, HD)
    queries = joined[:, :local_cols].reshape(head_shape)
    key_rows = joined[:, local_cols : 2 * local_cols].reshape(head_shape)
    values = joined[:, 2 * local_cols :].reshape(head_shape)
    context, log_total = attend_forward(queries, key_rows, values, factor)
    context = context.reshape(group_rows, local_cols).astype(jnp.bfloat16)
    branch = (
        lax.psum_scatter(
            product(context, w_out).astype(jnp.bfloat16), "tp", scatter_dimension=0, tiled=True
        ).astype(jnp.float32)
        + b_out
    )
    middle = initial + scale_one * branch
    normed_two = layer_norm(middle, gain_two, shift_two).astype(jnp.bfloat16)
    gathered_two = lax.all_gather(normed_two, "tp", axis=0, tiled=True)
    pre_act = product(gathered_two, w_up) + b_up
    hidden = gelu_exact(pre_act).astype(jnp.bfloat16)
    output = (
        lax.psum_scatter(
            product(hidden, w_down).astype(jnp.bfloat16), "tp", scatter_dimension=0, tiled=True
        ).astype(jnp.float32)
        + b_down
    )
    block_out = (middle + scale_two * output).astype(jnp.bfloat16)
    grad_block = cotangent.astype(jnp.float32) * chosen.astype(jnp.float32)
    grad_output = (scale_two * grad_block).astype(jnp.bfloat16)
    grad_scale_two = jnp.sum(grad_block * output, axis=0)
    grad_b_down = jnp.sum(grad_output.astype(jnp.float32), axis=0)
    portion = lax.all_gather(grad_output, "tp", axis=0, tiled=True)
    grad_hidden = times_transposed(portion, w_down)
    grad_w_down = transposed_times(hidden, portion)
    grad_hidden, grad_w_down = (grad_hidden, grad_w_down)
    unused, gelu_pull = jax.vjp(gelu_exact, pre_act)
    grad_pre = gelu_pull(grad_hidden)[0].astype(jnp.bfloat16)
    grad_b_up = jnp.sum(grad_pre.astype(jnp.float32), axis=0)
    grad_normed_two = lax.psum_scatter(
        times_transposed(grad_pre, w_up).astype(jnp.bfloat16), "tp", scatter_dimension=0, tiled=True
    ).astype(jnp.float32)
    grad_w_up = transposed_times(lax.all_gather(normed_two, "tp", axis=0, tiled=True), grad_pre)
    grad_middle_norm, grad_gain_two, grad_shift_two = norm_backward(
        middle, gain_two, shift_two, grad_normed_two
    )
    grad_middle = grad_block + grad_middle_norm
    grad_branch = (scale_one * grad_middle).astype(jnp.bfloat16)
    grad_scale_one = jnp.sum(grad_middle * branch, axis=0)
    grad_b_out = jnp.sum(grad_branch.astype(jnp.float32), axis=0)
    portion = lax.all_gather(grad_branch, "tp", axis=0, tiled=True)
    grad_context = times_transposed(portion, w_out)
    grad_w_out = transposed_times(context, portion)
    grad_context, grad_w_out = (grad_context, grad_w_out)
    grad_context = grad_context.astype(jnp.bfloat16).reshape(head_shape)
    grad_queries, grad_keys, grad_values = attend_backward(
        queries, key_rows, values, log_total, grad_context, factor
    )
    grad_joined = jnp.concatenate(
        [
            grad_queries.reshape(group_rows, local_cols),
            grad_keys.reshape(group_rows, local_cols),
            grad_values.reshape(group_rows, local_cols),
        ],
        axis=1,
    ).astype(jnp.bfloat16)
    grad_b_query = jnp.sum(grad_joined[:, :local_cols].astype(jnp.float32), axis=0)
    grad_b_value = jnp.sum(grad_joined[:, 2 * local_cols :].astype(jnp.float32), axis=0)
    grad_normed = lax.psum_scatter(
        times_transposed(grad_joined, w_joined).astype(jnp.bfloat16),
        "tp",
        scatter_dimension=0,
        tiled=True,
    ).astype(jnp.float32)
    grad_w_joined = transposed_times(lax.all_gather(normed, "tp", axis=0, tiled=True), grad_joined)
    grad_initial_norm, grad_gain_one, grad_shift_one = norm_backward(
        initial, gain_one, shift_one, grad_normed
    )
    grad_initial = grad_middle + grad_initial_norm
    grad_tokens = jnp.where(chosen, 0.0, grad_initial)
    grad_mask_token = jnp.sum(jnp.where(chosen, grad_initial, 0.0), axis=0)
    (
        grad_mask_token,
        grad_gain_one,
        grad_shift_one,
        grad_b_out,
        grad_scale_one,
        grad_gain_two,
        grad_shift_two,
        grad_b_down,
        grad_scale_two,
    ) = lax.psum(
        (
            grad_mask_token,
            grad_gain_one,
            grad_shift_one,
            grad_b_out,
            grad_scale_one,
            grad_gain_two,
            grad_shift_two,
            grad_b_down,
            grad_scale_two,
        ),
        ("dp", "tp"),
    )
    grad_b_query, grad_b_value, grad_b_up = lax.psum((grad_b_query, grad_b_value, grad_b_up), "dp")
    grad_w_joined, grad_w_out, grad_w_up, grad_w_down = (
        lax.psum_scatter(
            grad_w_joined.astype(jnp.bfloat16), "dp", scatter_dimension=0, tiled=True
        ).astype(jnp.float32),
        lax.psum_scatter(
            grad_w_out.astype(jnp.bfloat16), "dp", scatter_dimension=1, tiled=True
        ).astype(jnp.float32),
        lax.psum_scatter(
            grad_w_up.astype(jnp.bfloat16), "dp", scatter_dimension=0, tiled=True
        ).astype(jnp.float32),
        lax.psum_scatter(
            grad_w_down.astype(jnp.bfloat16), "dp", scatter_dimension=1, tiled=True
        ).astype(jnp.float32),
    )
    grad_w_query = grad_w_joined[:, :local_cols]
    grad_w_key = grad_w_joined[:, local_cols : 2 * local_cols]
    grad_w_value = grad_w_joined[:, 2 * local_cols :]
    return (
        block_out,
        grad_tokens,
        grad_mask_token,
        grad_gain_one,
        grad_shift_one,
        grad_w_query,
        grad_w_key,
        grad_w_value,
        grad_b_query,
        grad_b_value,
        grad_w_out,
        grad_b_out,
        grad_scale_one,
        grad_gain_two,
        grad_shift_two,
        grad_w_up,
        grad_b_up,
        grad_w_down,
        grad_b_down,
        grad_scale_two,
    )


def solution(mesh):
    placed = (
        P(("dp", "tp"), None),
        P(("dp", "tp")),
        P(("dp", "tp"), None),
        P(),
        P(),
        P(),
        P(None, "tp"),
        P(None, "tp"),
        P(None, "tp"),
        P("tp"),
        P("tp"),
        P("tp", None),
        P(),
        P(),
        P(),
        P(),
        P(None, "tp"),
        P("tp"),
        P("tp", None),
        P(),
        P(),
    )
    return jax.shard_map(
        body,
        mesh=mesh,
        in_specs=placed,
        out_specs=(
            P(("dp", "tp"), None),
            P(("dp", "tp"), None),
            P(),
            P(),
            P(),
            P("dp", "tp"),
            P("dp", "tp"),
            P("dp", "tp"),
            P("tp"),
            P("tp"),
            P("tp", "dp"),
            P(),
            P(),
            P(),
            P(),
            P("dp", "tp"),
            P("tp"),
            P("tp", "dp"),
            P(),
            P(),
        ),
        check_vma=False,
    )
```

profile of v0, /device:TPU:0, one launch (start us, length us, event | category | flops | bytes accessed | tf_op | source)
XLA Modules:
  0.0 685.6 jit_solution(13079850631504761603)
XLA Ops:
  14.5 3.0 fusion.36
  22.1 7.4 %all-gather.9.cloned.1.call-done = bf16[2,788,1024]{2,1,0:T(8,128)(2,1)} async-done(((bf16[1,788,1024]{2,1,0:T(8,128)(2,1)}), bf16[2,788,1024]{2,1,0:T(8,128)(2,1)}) %all-gather.9.cloned.1.call-update) | async-done | bytes 3227664 | tf_op jit(solution)/shard_map/all_gather | solution.py:118
  29.5 4.2 reshape.159
  33.7 8.1 %add_convert_fusion.1 = bf16[1576,1536]{1,0:T(8,128)(2,1)S(1)} fusion(bf16[1576,1024]{1,0:T(8,128)(2,1)} %reshape.159, bf16[1024,1536]{1,0:T(8,128)(2,1)} %copy-done.28, f32[1536]{0:T(1024)S(1)} %pad_maximum_fusion), kind=kOutput, calls=%fused_computation.25 | convolution fusion | flops 4962508800 | bytes 11220992 | tf_op jit(solution)/shard_map/dot_general | solution.py:31
  41.8 2.3 fusion.46
  44.1 5.3 reshape.172
  49.4 4.8 copy.77
  54.2 5.3 reshape.171
  59.5 4.8 copy.76
  64.3 5.3 reshape.170
  69.6 4.8 copy.78
  74.4 4.2 multiply_reduce_fusion.1
  78.6 3.3 fusion.10
  83.5 5.8 convert_bitcast_fusion.1
  89.3 2.6 copy.80
  91.9 4.6 convert_element_type.125
  96.5 5.0 convolution_convert_fusion.6
  101.5 8.2 %fusion = bf16[792,1024]{1,0:T(8,128)(2,1)} fusion(bf16[1576,1024]{1,0:T(8,128)(2,1)} %convolution_convert_fusion.6), kind=kCustom, calls=%all-reduce-scatter | all-reduce-scatter fusion | flops 1622017 | bytes 4850176
  113.9 9.2 %concatenate.13 = bf16[796,1024]{1,0:T(8,128)(2,1)} concatenate(bf16[4,1024]{1,0:T(4,128)(2,1)S(1)} %collective-permute-done, bf16[792,1024]{1,0:T(8,128)(2,1)} %fusion), dimensions={0} | concatenate | bytes 3260416
  123.2 2.9 fusion.42
  127.8 2.8 fusion.34
  130.7 4.3 reshape.163
  135.0 9.2 %all-gather.11.cloned.1.call-done = bf16[2,788,1024]{2,1,0:T(8,128)(2,1)} async-done(((bf16[1,788,1024]{2,1,0:T(8,128)(2,1)}), bf16[2,788,1024]{2,1,0:T(8,128)(2,1)}) %all-gather.11.cloned.1.call-update) | async-done | bytes 3227664 | tf_op jit(solution)/shard_map/all_gather | solution.py:135
  144.2 4.3 reshape.161
  148.5 10.2 %fusion.48 = f32[1576,2048]{1,0:T(8,128)S(1)} fusion(bf16[1576,1024]{1,0:T(8,128)(2,1)} %reshape.161, bf16[1024,2048]{1,0:T(8,128)(2,1)} %param.37), kind=kOutput, calls=%fused_computation.118 | convolution fusion | flops 6610223104 | bytes 20332544 | tf_op jit(solution)/shard_map/dot_general | solution.py:31
  158.7 38.5 %convert_reduce_fusion = (f32[2048]{0:T(1024)}, bf16[1576,2048]{1,0:T(8,128)(2,1)S(1)}, f32[1576,2048]{1,0:T(8,128)}) fusion(f32[1576,2048]{1,0:T(8,128)S(1)} %fusion.48, f32[2048]{0:T(1024)S(1)} %copy-done.47, bf16[1576,1024]{1,0:T(8,128)(2,1)S(1)} %copy-done.20, bf16[2048,1024]{1,0:T(8,128)(2,1)S(1)} %copy-done.55), kind=kOutput, calls=%fused_computation.7 | convolution fusion | flops 6852294656 | bytes 39714816 | tf_op jit(solution)/shard_map/dot_general | solution.py:35
  197.2 2.7 copy-done.56
  199.9 8.6 %convolution_convert_fusion.4 = bf16[1576,1024]{1,0:T(8,128)(2,1)} fusion(bf16[1576,2048]{1,0:T(8,128)(2,1)S(1)} %get-tuple-element.47, bf16[1024,2048]{1,0:T(8,128)(2,1)S(1)} %copy-done.54), kind=kOutput, calls=%fused_computation.49 | convolution fusion | flops 6611836928 | bytes 13877248 | tf_op jit(solution)/shard_map/dot_general | solution.py:35
  208.5 8.1 %fusion.2 = bf16[792,1024]{1,0:T(8,128)(2,1)} fusion(bf16[1576,1024]{1,0:T(8,128)(2,1)} %convolution_convert_fusion.4), kind=kCustom, calls=%all-reduce-scatter.2 | all-reduce-scatter fusion | flops 1622017 | bytes 4850176
  220.3 9.4 %concatenate.15 = bf16[796,1024]{1,0:T(8,128)(2,1)} concatenate(bf16[4,1024]{1,0:T(4,128)(2,1)S(1)} %collective-permute-done.2, bf16[792,1024]{1,0:T(8,128)(2,1)} %fusion.2), dimensions={0} | concatenate | bytes 3260416
  229.7 4.3 fusion.22
  234.0 3.1 fusion.23
  237.2 4.1 multiply_reduce_fusion.3
  244.6 13.1 %multiply_convert_fusion.1 = bf16[1576,2048]{1,0:T(8,128)(2,1)} fusion(f32[1576,2048]{1,0:T(8,128)} %get-tuple-element.48, f32[1576,2048]{1,0:T(8,128)} %copy-done.17, f32[2048]{0:T(1024)S(1)} %copy-done.47), kind=kLoop, calls=%fused_computation.9 | loop fusion | flops 12910592 | bytes 32284672 | tf_op jit(solution)/shard_map/convert_element_type | solution.py:137
  258.2 4.3 reshape.165
  262.5 5.0 convolution_convert_fusion.8
  267.6 13.3 %convolution_convert_fusion = bf16[2048,1024]{0,1:T(8,128)(2,1)} fusion(bf16[1576,2048]{1,0:T(8,128)(2,1)} %multiply_convert_fusion.1, bf16[1576,1024]{1,0:T(8,128)(2,1)} %reshape.163), kind=kOutput, calls=%fused_computation.45 | convolution fusion | flops 6612320256 | bytes 13877248 | tf_op jit(solution)/shard_map/dot_general | solution.py:41
  281.7 12.4 %convolution_convert_fusion.1 = bf16[1024,2048]{1,0:T(8,128)(2,1)} fusion(bf16[1576,1024]{1,0:T(8,128)(2,1)} %reshape.161, bf16[1576,2048]{1,0:T(8,128)(2,1)} %copy-done.56), kind=kOutput, calls=%fused_computation.46 | convolution fusion | flops 6612320256 | bytes 13877248 | tf_op jit(solution)/shard_map/dot_general | solution.py:41
  294.2 12.2 %convolution_convert_fusion.5 = bf16[1576,1024]{1,0:T(8,128)(2,1)} fusion(bf16[1576,2048]{1,0:T(8,128)(2,1)} %multiply_convert_fusion.1, bf16[2048,1024]{1,0:T(8,128)(2,1)} %param.39), kind=kOutput, calls=%fused_computation.50 | convolution fusion | flops 6611836928 | bytes 13877248 | tf_op jit(solution)/shard_map/dot_general | solution.py:31
  308.3 3.3 reshape.173
  311.6 3.7 copy.82
  315.3 8.0 %convert_bitcast_fusion = bf16[8,197,8,64]{1,3,2,0:T(8,128)(2,1)S(1)} fusion(bf16[8,197,8,64]{1,3,2,0:T(8,128)(2,1)S(1)} %copy.82, f32[8,8,197,197]{2,3,1,0:T(8,128)} %copy-done.1, f32[8,8,197]{2,1,0:T(8,128)S(1)} %log_add_fusion), kind=kOutput, calls=%fused_computation.81 | convolution fusion | flops 326181568 | bytes 13213184 | tf_op jit(solution)/shard_map/ihqk,iqhd->ikhd/dot_general | solution.py:78
  323.3 2.6 copy.92
  325.9 4.8 reshape.157
  330.7 14.2 %multiply_reduce_fusion = (f32[8,8,197]{2,1,0:T(8,128)S(1)}, f32[8,8,197,197]{2,3,1,0:T(8,128)}) fusion(f32[8,8,197,197]{2,3,1,0:T(8,128)} %copy-done.1, f32[8,8,197]{2,1,0:T(8,128)S(1)} %log_add_fusion, bf16[8,197,8,64]{1,3,2,0:T(8,128)(2,1)} %copy-done.14, bf16[8,197,8,64]{1,3,2,0:T(8,128)(2,1)} %copy.78), kind=kOutput, calls=%fused_computation.2 | convolution fusion | flops 327845824 | bytes 23198720 | tf_op jit(solution)/shard_map/iqhd,ikhd->ihqk/dot_general | solution.py:65
  345.0 6.7 multiply_convert_fusion
  351.7 2.7 copy-done.7
  355.8 2.6 copy.86
  358.4 4.6 reshape.155
  363.0 5.1 fusion.32
  369.4 3.9 reshape.156
  376.1 2.2 copy-done.27
  378.3 7.6 %convolution_convert_fusion.2 = bf16[1024,1536]{1,0:T(8,128)(2,1)} fusion(bf16[1576,1024]{1,0:T(8,128)(2,1)S(1)} %copy-done.19, bf16[1576,1536]{0,1:T(8,128)(2,1)S(1)} %constant_dynamic-update-slice_fusion.3), kind=kOutput, calls=%fused_computation.47 | convolution fusion | flops 4959240192 | bytes 11214848 | tf_op jit(solution)/shard_map/dot_general | solution.py:41
  385.9 10.2 %convolution_convert_fusion.3 = bf16[1576,1024]{1,0:T(8,128)(2,1)} fusion(bf16[1576,1536]{0,1:T(8,128)(2,1)} %copy-done.27, bf16[1024,1536]{1,0:T(8,128)(2,1)} %copy-done.28), kind=kOutput, calls=%fused_computation.48 | convolution fusion | flops 4959281152 | bytes 11214848 | tf_op jit(solution)/shard_map/dot_general | solution.py:35
  396.1 11.8 %fusion.43 = (bf16[792,1024]{1,0:T(8,128)(2,1)}, bf16[792,1024]{1,0:T(8,128)(2,1)}) fusion(bf16[1576,1024]{1,0:T(8,128)(2,1)} %convolution_convert_fusion.5, bf16[1576,1024]{1,0:T(8,128)(2,1)} %convolution_convert_fusion.3), kind=kCustom, calls=%all-reduce-scatter.4 | all-reduce-scatter fusion | flops 3244033 | bytes 9699840
  415.0 77.9 %all-reduce.9 = (f32[512]{0:T(512)}, f32[512]{0:T(512)}, f32[2048]{0:T(1024)}) all-reduce(f32[512]{0:T(512)S(1)} %convert_reduce_fusion.4, f32[512]{0:T(512)S(1)} %convert_reduce_fusion.3, f32[2048]{0:T(1024)S(1)} %copy-done.46), channel_id=1, replica_groups=mesh['dp'=16,'tp'=2] {'dp'}, use_global_device_ids=true, to_apply=%region_23.24 | all-reduce | flops 3072 | bytes 24576 | tf_op jit(solution)/shard_map/psum | solution.py:222
  493.0 9.3 %concatenate.16 = bf16[796,1024]{1,0:T(8,128)(2,1)} concatenate(bf16[4,1024]{1,0:T(4,128)(2,1)S(1)} %collective-permute-done.3, bf16[792,1024]{1,0:T(8,128)(2,1)} %get-tuple-element.45), dimensions={0} | concatenate | bytes 3260416
  502.2 9.2 %concatenate.14 = bf16[796,1024]{1,0:T(8,128)(2,1)} concatenate(bf16[4,1024]{1,0:T(4,128)(2,1)S(1)} %collective-permute-done.1, bf16[792,1024]{1,0:T(8,128)(2,1)} %get-tuple-element.44), dimensions={0} | concatenate | bytes 3260416
  511.5 3.1 fusion.21
  514.6 3.6 fusion.24
  518.3 8.0 %multiply_reduce_fusion.2 = (f32[1024]{0:T(1024)S(1)}, f32[1024]{0:T(1024)S(1)}, bf16[788,1024]{1,0:T(8,128)(2,1)}, f32[1024]{0:T(1024)S(1)}, f32[788,1024]{1,0:T(8,128)}) fusion(bf16[788,1024]{1,0:T(8,128)(2,1)} %param.23, f32[788]{0:T(1024)S(1)} %copy-done.36, f32[1024]{0:T(1024)S(1)} %copy-done.49, bf16[796,1024]{1,0:T(8,128)(2,1)} %concatenate.14, ...), kind=kLoop, calls=%fused_computation.58 | loop fusion | flops 24204288 | bytes 16191656 | tf_op jit(solution)/shard_map/reduce_sum | solution.py:147
  526.3 39.7 %all-reduce.8 = (f32[1024]{0:T(1024)}, f32[1024]{0:T(1024)}, f32[1024]{0:T(1024)}, f32[1024]{0:T(1024)}, f32[1024]{0:T(1024)}, /*index=5*/f32[1024]{0:T(1024)}, f32[1024]{0:T(1024)}, f32[1024]{0:T(1024)}, f32[1024]{0:T(1024)}) all-reduce(f32[1024]{0:T(1024)S(1)} %get-tuple-element.58, ...), channel_id=1, replica_groups=mesh['dp'=16,'tp'=2] {'dp','tp'}, use_global_device_ids=true, to_apply=%region_16.17 | all-reduce | flops 9216 | bytes 73728 | tf_op jit(solution)/shard_map/psum | solution.py:208
  566.0 4.0 broadcast_select_fusion
  575.0 101.9 %reduce-scatter.13.cloned.1.call-done = bf16[64,1536]{1,0:T(8,128)(2,1)} async-done(((bf16[1024,1536]{1,0:T(8,128)(2,1)}), bf16[64,1536]{1,0:T(8,128)(2,1)}) %reduce-scatter.13.cloned.1.call-update) | async-done | bytes 196624 | tf_op jit(solution)/shard_map/reduce_scatter | solution.py:224
  (186 shorter events, 48.1 us)
Async XLA Ops:
  7.2 89.3 %copy-start = (bf16[512,1024]{1,0:T(8,128)(2,1)S(1)}, bf16[512,1024]{1,0:T(8,128)(2,1)}, u32[]{:S(2)}) copy-start(bf16[512,1024]{1,0:T(8,128)(2,1)} %param.32) | copy-start | bytes 3145732
  7.2 5.1 copy-start.24
  7.2 5.1 copy-start.2
  7.2 5.1 copy-start.38
  7.2 5.1 copy-start.48
  7.3 22.3 %all-gather.9.cloned.1.call-start = ((), (), s32[]{:S(2)}) async-start(), calls=%async_computation.8 | async-start | bytes 4866048 | tf_op jit(solution)/shard_map/all_gather | solution.py:118
  8.1 6.3 copy-start.35
  10.1 4.3 copy-start.33
  10.1 4.3 copy-start.44
  12.3 5.2 copy-start.42
  12.4 5.1 copy-start.40
  14.4 116.3 %all-gather.13.cloned.1.call-start = ((), (), s32[]{:S(2)}) async-start(), calls=%async_computation.10 | async-start | bytes 4866048 | tf_op jit(solution)/shard_map/all_gather | solution.py:149
  17.5 4.5 copy-start.51
  17.6 4.5 copy-start.52
  17.6 126.7 %all-gather.11.cloned.1.call-start = ((), (), s32[]{:S(2)}) async-start(), calls=%async_computation.9 | async-start | bytes 4866048 | tf_op jit(solution)/shard_map/all_gather | solution.py:135
  78.6 4.7 copy-start.1
  78.6 4.9 copy-start.25
  83.5 5.8 copy-start.30
  101.5 11.1 %copy-start.53 = (u32[32]{0:T(128)S(1)}, u32[32]{0:T(128)}, u32[]{:S(2)}) copy-start(u32[32]{0:T(128)} %constant.90) | copy-start | bytes 388
  101.5 21.6 %copy-start.29 = (f32[1024]{0:T(1024)S(1)}, f32[1024]{0:T(1024)}, u32[]{:S(2)}) copy-start(f32[1024]{0:T(1024)} %param.34) | copy-start | bytes 12292
  101.5 21.6 %copy-start.32 = (f32[1024]{0:T(1024)S(1)}, f32[1024]{0:T(1024)}, u32[]{:S(2)}) copy-start(f32[1024]{0:T(1024)} %param.33) | copy-start | bytes 12292
  110.5 3.5 collective-permute-start
  123.2 3.0 copy-start.4
  123.2 4.6 copy-start.37
  123.2 4.6 copy-start.50
  130.6 127.5 %all-gather.15.cloned.1.call-start = ((), (), s32[]{:S(2)}) async-start(), calls=%async_computation.11 | async-start | bytes 4866048 | tf_op jit(solution)/shard_map/all_gather | solution.py:167
  148.5 10.2 %copy-start.20 = (bf16[1576,1024]{1,0:T(8,128)(2,1)S(1)}, bf16[1576,1024]{1,0:T(8,128)(2,1)}, u32[]{:S(2)}) copy-start(bf16[1576,1024]{1,0:T(8,128)(2,1)} %reshape.163) | copy-start | bytes 9682948
  148.5 10.2 %copy-start.47 = (f32[2048]{0:T(1024)S(1)}, f32[2048]{0:T(1024)}, u32[]{:S(2)}) copy-start(f32[2048]{0:T(1024)} %param.38) | copy-start | bytes 24580
  148.5 10.2 %copy-start.55 = (bf16[2048,1024]{1,0:T(8,128)(2,1)S(1)}, bf16[2048,1024]{1,0:T(8,128)(2,1)}, u32[]{:S(2)}) copy-start(bf16[2048,1024]{1,0:T(8,128)(2,1)} %param.39) | copy-start | bytes 12582916
  158.7 38.5 %copy-start.17 = (f32[1576,2048]{1,0:T(8,128)}, f32[1576,2048]{1,0:T(8,128)S(1)}, u32[]{:S(2)}) copy-start(f32[1576,2048]{1,0:T(8,128)S(1)} %fusion.48) | copy-start | bytes 38731780
  158.7 41.2 %copy-start.54 = (bf16[1024,2048]{1,0:T(8,128)(2,1)S(1)}, bf16[1024,2048]{1,0:T(8,128)(2,1)}, u32[]{:S(2)}) copy-start(bf16[1024,2048]{1,0:T(8,128)(2,1)} %param.37) | copy-start | bytes 12582916
  217.2 3.0 collective-permute-start.2
  229.7 4.3 copy-start.5
  229.7 4.3 copy-start.11
  233.9 3.2 copy-start.16
  234.0 3.2 copy-start.36
  244.6 325.4 %reduce-scatter.15.cloned.1.call-start = ((), (), s32[]{:S(2)}) async-start(), calls=%async_computation.5 | async-start | bytes 1114112 | tf_op jit(solution)/shard_map/reduce_scatter | solution.py:227
  257.8 4.7 copy-start.22
  267.5 303.9 %reduce-scatter.19.cloned.1.call-start = ((), (), s32[]{:S(2)}) async-start(), calls=%async_computation.7 | async-start | bytes 4456448 | tf_op jit(solution)/shard_map/reduce_scatter | solution.py:233
  280.9 292.4 %reduce-scatter.17.cloned.1.call-start = ((), (), s32[]{:S(2)}) async-start(), calls=%async_computation.6 | async-start | bytes 4456448 | tf_op jit(solution)/shard_map/reduce_scatter | solution.py:230
  294.1 382.8 %reduce-scatter.13.cloned.1.call-start = ((), (), s32[]{:S(2)}) async-start(), calls=%async_computation.4 | async-start | bytes 3342336 | tf_op jit(solution)/shard_map/reduce_scatter | solution.py:224
  294.2 12.2 %copy-start.21 = (bf16[1576,1024]{1,0:T(8,128)(2,1)S(1)}, bf16[1576,1024]{1,0:T(8,128)(2,1)}, u32[]{:S(2)}) copy-start(bf16[1576,1024]{1,0:T(8,128)(2,1)} %reshape.165) | copy-start | bytes 9682948
  315.3 8.0 %copy-start.14 = (bf16[8,197,8,64]{1,3,2,0:T(8,128)(2,1)}, bf16[8,197,8,64]{1,3,2,0:T(8,128)(2,1)S(1)}, u32[]{:S(2)}) copy-start(bf16[8,197,8,64]{1,3,2,0:T(8,128)(2,1)S(1)} %copy.82) | copy-start | bytes 4841476
  325.9 19.1 %slice-start = ((s8[13107200]{0:T(1024)(128)(4,1)}), s8[524288]{0:T(1024)(128)(4,1)S(1)}, s32[]{:S(2)}) async-start(s8[13107200]{0:T(1024)(128)(4,1)} %bitcast.76), calls=%async_computation.12 | async-start | bytes 1048576
  330.7 14.3 %slice-start.1 = ((s8[13107200]{0:T(1024)(128)(4,1)}), s8[4194304]{0:T(1024)(128)(4,1)S(1)}, s32[]{:S(2)}) async-start(s8[13107200]{0:T(1024)(128)(4,1)} %bitcast.76), calls=%async_computation.13 | async-start | bytes 8388608
  330.7 14.3 %slice-start.2 = ((s8[13107200]{0:T(1024)(128)(4,1)}), s8[4194304]{0:T(1024)(128)(4,1)S(1)}, s32[]{:S(2)}) async-start(s8[13107200]{0:T(1024)(128)(4,1)} %bitcast.76), calls=%async_computation.14 | async-start | bytes 8388608
  330.7 14.2 %slice-start.3 = ((s8[13107200]{0:T(1024)(128)(4,1)}), s8[4194304]{0:T(1024)(128)(4,1)S(1)}, s32[]{:S(2)}) async-start(s8[13107200]{0:T(1024)(128)(4,1)} %bitcast.76), calls=%async_computation.15 | async-start | bytes 8388608
  345.0 9.5 %copy-start.12 = (bf16[8,197,8,64]{1,3,2,0:T(8,128)(2,1)S(1)}, bf16[8,197,8,64]{1,3,2,0:T(8,128)(2,1)}, u32[]{:S(2)}) copy-start(bf16[8,197,8,64]{1,3,2,0:T(8,128)(2,1)} %copy.77) | copy-start | bytes 4841476
  351.7 2.7 copy-start.7
  355.8 7.2 %copy-start.13 = (bf16[8,197,8,64]{1,3,2,0:T(8,128)(2,1)S(1)}, bf16[8,197,8,64]{1,3,2,0:T(8,128)(2,1)}, u32[]{:S(2)}) copy-start(bf16[8,197,8,64]{1,3,2,0:T(8,128)(2,1)} %copy.76) | copy-start | bytes 4841476
  375.3 3.0 copy-start.19
  407.9 7.0 %copy-start.46 = (f32[2048]{0:T(1024)S(1)}, f32[2048]{0:T(1024)}, u32[]{:S(2)}) copy-start(f32[2048]{0:T(1024)} %get-tuple-element.46) | copy-start | bytes 24580
  409.4 83.5 %collective-permute-start.3 = (bf16[4,1024]{1,0:T(4,128)(2,1)S(1)}, bf16[4,1024]{1,0:T(4,128)(2,1)S(1)}, u32[]{:S(2)}, u32[]{:S(2)}) collective-permute-start(bf16[4,1024]{1,0:T(4,128)(2,1)S(1)} %slice.35), channel_id=1, source_target_pairs={{0,1},{2,3},{4,5},{6,7},{8,9},{10,11},{12,13},{14,15},{16,17},{18,... | collective-permute-start | bytes 24584
  411.6 90.6 %collective-permute-start.1 = (bf16[4,1024]{1,0:T(4,128)(2,1)S(1)}, bf16[4,1024]{1,0:T(4,128)(2,1)S(1)}, u32[]{:S(2)}, u32[]{:S(2)}) collective-permute-start(bf16[4,1024]{1,0:T(4,128)(2,1)S(1)} %slice.33), channel_id=1, source_target_pairs={{0,1},{2,3},{4,5},{6,7},{8,9},{10,11},{12,13},{14,15},{16,17},{18,... | collective-permute-start | bytes 24584
  492.9 18.5 %copy-start.3 = (bf16[788,1024]{1,0:T(8,128)(2,1)S(1)}, bf16[788,1024]{1,0:T(8,128)(2,1)}, u32[]{:S(2)}) copy-start(bf16[788,1024]{1,0:T(8,128)(2,1)} %param.21) | copy-start | bytes 4841476
  493.0 18.5 %copy-start.34 = (f32[788]{0:T(1024)S(1)}, f32[788]{0:T(1024)}, u32[]{:S(2)}) copy-start(f32[788]{0:T(1024)} %copy-done.33) | copy-start | bytes 9460
  493.0 18.5 %copy-start.39 = (f32[1024]{0:T(1024)S(1)}, f32[1024]{0:T(1024)}, u32[]{:S(2)}) copy-start(f32[1024]{0:T(1024)} %param.25) | copy-start | bytes 12292
  502.2 12.4 %copy-start.43 = (f32[788]{0:T(1024)S(1)}, f32[788]{0:T(1024)}, u32[]{:S(2)}) copy-start(f32[788]{0:T(1024)} %copy-done.42) | copy-start | bytes 9460
  502.2 12.4 %copy-start.41 = (f32[788]{0:T(1024)S(1)}, f32[788]{0:T(1024)}, u32[]{:S(2)}) copy-start(f32[788]{0:T(1024)} %copy-done.40) | copy-start | bytes 9460
  511.5 6.8 copy-start.6
  511.5 6.8 copy-start.9
  511.5 6.7 copy-start.10
  511.5 6.7 copy-start.45
  511.5 6.7 copy-start.49
  (9 other events, 17.2 us)
Sparse Core Ops, SparseCore 0:
  14.5 14.9 all-gather.8
  31.0 13.4 all-gather.12
  130.8 13.4 all-gather.10
  244.7 13.4 all-gather.14
  267.6 78.8 reduce-scatter.14
  348.8 92.3 reduce-scatter.18
  443.6 97.0 reduce-scatter.16
  546.5 130.4 reduce-scatter.12
where the time goes:
time: 692 us; the launch traced here: 686 us
  matrix products  171 us (25%)
  blocking collectives  146 us (21%)
  local copies, waits for them, and re-layouts  145 us (21%)
  waiting for transfers between devices  120 us (17%)
  other arithmetic  79.4 us (11%)
  between operations  15.8 us (2%)
  starting transfers between devices  8.21 us (1%)
    reduce_scatter x1, waiting for transfers between devices, body(): lax.psum_scatter(grad_w_joined.astype(jnp.bfloat16), 'dp', scatter_dimens...  102 us
    psum x1, blocking collectives, body(): lax.psum((grad_b_query, grad_b_value, grad_b_up), 'dp')  77.9 us
    unnamed x139, local copies, waits for them, and re-layouts  76.5 us
    dot_general x4, matrix products, times_transposed(): lax.dot_general(left, right, (((1,), (1,)), ((), ())), preferred_element_...  59.2 us
    psum x1, blocking collectives, body(): lax.psum((grad_mask_token, grad_gain_one, grad_shift_one, grad_b_out, gra...  39.7 us
    dot_general x4, matrix products, transposed_times(): lax.dot_general(left, right, (((0,), (0,)), ((), ())), preferred_element_...  38.2 us
    dot_general x4, matrix products, product(): return jnp.dot(left, right, preferred_element_type=jnp.float32)  35.5 us
    unnamed x3, blocking collectives  28.1 us
  transfers between devices with their start and end apart: 12, of which 5 were waited for; matrix products, arithmetic and copies ran while one was open for 44% of the time, Pallas kernels for 0%

commit v1 on v0

--- a/solution.py
+++ b/solution.py
@@ -1,16 +1,21 @@
+import functools
 import math
 
 import jax
 import jax.numpy as jnp
 from jax import lax
+from jax.experimental import pallas as pl
+from jax.experimental.pallas import tpu as pltpu
 from jax.sharding import PartitionSpec as P
 
 SEQ = 197
 HD = 64
-
-
+PAIR = 2 * HD
 EPSILON = 1e-06
-
+BF16 = jnp.bfloat16
+F32 = jnp.float32
+MIB = 2**20
+LOWEST = -1e30
 
 def layer_norm(rows_in, gain_vec, shift_vec):
     center = rows_in - jnp.mean(rows_in, axis=-1, keepdims=True)
@@ -84,7 +89,7 @@
     return (grad_queries, grad_keys, grad_values)
 
 
-def body(
+def gathered_body(
     tokens,
     masked,
     cotangent,
@@ -261,6 +266,619 @@
     )
 
 
+def nn(left, right):
+    return lax.dot_general(left, right, (((1,), (0,)), ((), ())), preferred_element_type=F32)
+
+
+def nt(left, right):
+    return lax.dot_general(left, right, (((1,), (1,)), ((), ())), preferred_element_type=F32)
+
+
+def tn(left, right):
+    return lax.dot_general(left, right, (((0,), (0,)), ((), ())), preferred_element_type=F32)
+
+
+def padded(rows):
+    return -(-rows // 32) * 32
+
+
+def windows(rows):
+    found = []
+    for image in range(rows // SEQ):
+        first = image * SEQ
+        start = first // 16 * 16
+        found.append((start, -(-(first - start + SEQ) // 16) * 16, first - start))
+    return found
+
+
+def row_blocks(total, size=160):
+    return [slice(s, min(s + size, total)) for s in range(0, total, size)]
+
+
+def inside(shape, axis, offset):
+    at = lax.broadcasted_iota(jnp.int32, shape, axis)
+    return (at >= offset) & (at < offset + SEQ)
+
+
+def col_sum(values):
+    return jnp.sum(values, axis=0, keepdims=True)
+
+
+def row_mean(values):
+    return jnp.mean(values, axis=-1, keepdims=True)
+
+
+def moments(rows_in):
+    center = rows_in - row_mean(rows_in)
+    return center, lax.rsqrt(row_mean(center * center) + EPSILON)
+
+
+def norm_pull(rows_in, gain, grad):
+    center, inv = moments(rows_in)
+    hat = center * inv
+    scaled = grad * gain
+    back = (scaled - row_mean(scaled) - hat * row_mean(scaled * hat)) * inv
+    return back, col_sum(grad * hat), col_sum(grad)
+
+
+def gelu_parts(v):
+    size = jnp.abs(v)
+    t = 1.0 / (1.0 + (0.3275911 * 0.7071067811865476) * size)
+    e = jnp.exp(-0.5 * v * v)
+    tail = (
+        t
+        * (
+            0.5 * 0.254829592
+            + t
+            * (
+                0.5 * -0.284496736
+                + t * (0.5 * 1.421413741 + t * (0.5 * -1.453152027 + t * (0.5 * 1.061405429)))
+            )
+        )
+        * e
+    )
+    return jnp.where(v < 0, tail, 1.0 - tail), v * e * 0.3989422804014327
+
+
+def attend(rows, q_ref, k_ref, v_ref, ctx_ref):
+    ctx_ref[padded(rows) - 32 :, :] = jnp.zeros((32, ctx_ref.shape[1]), BF16)
+
+    def one_pair(pair, carry):
+        lanes = pl.ds(pl.multiple_of(pair * PAIR, PAIR), PAIR)
+        for start, size, offset in windows(rows):
+            win = slice(start, start + size)
+            q, k, v = q_ref[win, lanes], k_ref[win, lanes], v_ref[win, lanes]
+            low_half = lax.broadcasted_iota(jnp.int32, (size, PAIR), 1) < HD
+            here = inside((size, size), 1, offset)
+            total = None
+            for mine in (low_half, ~low_half):
+                zero = jnp.zeros_like(k)
+                scores = jnp.where(here, nt(q, jnp.where(mine, k, zero)), LOWEST)
+                raised = jnp.exp(scores - jnp.max(scores, axis=-1, keepdims=True))
+                share = 1.0 / jnp.sum(raised, axis=-1, keepdims=True)
+                part = nn((raised * share).astype(BF16), jnp.where(mine, v, zero))
+                total = part if total is None else total + part
+            keep = inside((size, PAIR), 0, offset)
+            ctx_ref[win, lanes] = jnp.where(keep, total.astype(BF16), ctx_ref[win, lanes])
+        return carry
+
+    lax.fori_loop(0, q_ref.shape[1] // PAIR, one_pair, 0)
+
+
+def project(normed_ref, wq_ref, wk_ref, wv_ref, bq_ref, bv_ref, q_ref, k_ref, v_ref):
+    normed = normed_ref[...]
+    q_ref[...] = (nn(normed, wq_ref[...]) + bq_ref[...]).astype(BF16) * BF16(1.0 / math.sqrt(HD))
+    k_ref[...] = nn(normed, wk_ref[...]).astype(BF16)
+    v_ref[...] = (nn(normed, wv_ref[...]) + bv_ref[...]).astype(BF16)
+
+
+def first_kernel(
+    rows, tok_ref, mask_ref, mt_ref, gain_ref, shift_ref, wq_ref, wk_ref, wv_ref, bq_ref, bv_ref,
+    normed_ref, q_ref, k_ref, v_ref, ctx_ref,
+):
+    for block in row_blocks(rows):
+        initial = jnp.where(mask_ref[block] > 0, mt_ref[...], tok_ref[block].astype(F32))
+        center, inv = moments(initial)
+        normed_ref[block] = (center * inv * gain_ref[...] + shift_ref[...]).astype(BF16)
+    over = padded(rows) - rows
+    normed_ref[rows:] = jnp.zeros((over, normed_ref.shape[1]), BF16)
+    project(normed_ref, wq_ref, wk_ref, wv_ref, bq_ref, bv_ref, q_ref, k_ref, v_ref)
+    attend(rows, q_ref, k_ref, v_ref, ctx_ref)
+
+
+def second_kernel(
+    rows, normed_ref, wq_ref, wk_ref, wv_ref, bq_ref, bv_ref, ctx_ref, wo_ref, wo2_ref, bo_ref,
+    s1_ref, gain_ref, shift_ref, tok_ref, mask_ref, mt_ref, cot_ref, s2_ref,
+    q_ref, k_ref, v_ref, ctx2_ref, middle_ref, normed2_ref, go_ref, sums_ref,
+):
+    project(normed_ref, wq_ref, wk_ref, wv_ref, bq_ref, bv_ref, q_ref, k_ref, v_ref)
+    attend(rows, q_ref, k_ref, v_ref, ctx2_ref)
+    over = padded(rows) - rows
+    width = middle_ref.shape[1]
+    total = jnp.zeros((1, width), F32)
+    for block in row_blocks(rows):
+        branch = nn(ctx_ref[block], wo_ref[...]) + nn(ctx2_ref[block], wo2_ref[...]) + bo_ref[...]
+        masked = mask_ref[block] > 0
+        initial = jnp.where(masked, mt_ref[...], tok_ref[block].astype(F32))
+        middle = initial + s1_ref[...] * branch
+        middle_ref[block] = middle
+        center, inv = moments(middle)
+        normed2_ref[block] = (center * inv * gain_ref[...] + shift_ref[...]).astype(BF16)
+        grad_out = (jnp.where(masked, cot_ref[block].astype(F32), 0.0) * s2_ref[...]).astype(BF16)
+        go_ref[block] = grad_out
+        total += col_sum(grad_out.astype(F32))
+    sums_ref[...] = total
+    normed2_ref[rows:] = jnp.zeros((over, width), BF16)
+    go_ref[rows:] = jnp.zeros((over, width), BF16)
+
+
+def feed_kernel(
+    me_ref, n2_ref, go_ref, wu_ref, wd_ref, bu_ref, hidden_ref, gp_ref, gwd_ref, gwu_ref, gb_ref
+):
+    pre = nn(n2_ref[...], wu_ref[...]) + bu_ref[...]
+    grad_hidden = nt(go_ref[...], wd_ref[...])
+    cdf, slope = gelu_parts(pre)
+    hidden = (pre * cdf).astype(BF16)
+    grad_pre = (grad_hidden * (cdf + slope)).astype(BF16)
+    hidden_ref[...] = hidden
+    gp_ref[...] = grad_pre
+    gb_ref[...] = col_sum(grad_pre.astype(F32))
+    store_blocks(me_ref[0], tn(go_ref[...], hidden), gwd_ref, 0)
+    store_blocks(me_ref[0], tn(n2_ref[...], grad_pre), gwu_ref, 0)
+
+
+def store_blocks(me, product_rows, out_ref, at):
+    parts, size, _ = out_ref.shape
+    cols = product_rows.shape[1]
+    for b in range(parts):
+        out_ref[b ^ me, :, at : at + cols] = product_rows[b * size : (b + 1) * size].astype(BF16)
+
+
+def middle_kernel(
+    rows, count, *refs
+):
+    gps, wus = refs[:count], refs[count : 2 * count]
+    (middle_ref, tok_ref, mask_ref, mt_ref, cot_ref, gain_ref, s1_ref) = refs[2 * count : 2 * count + 7]
+    gm_ref, gbr_ref, sums_ref, acc_ref = refs[2 * count + 7 :]
+    step = pl.program_id(0)
+    part = None
+    for gp_ref, wu_ref in zip(gps, wus):
+        one = nt(gp_ref[...], wu_ref[...])
+        part = one if part is None else part + one
+
+    @pl.when(step == 0)
+    def first():
+        acc_ref[...] = part
+
+    @pl.when(step > 0)
+    def later():
+        acc_ref[...] += part
+
+    @pl.when(step == pl.num_programs(0) - 1)
+    def last():
+        width = gm_ref.shape[1]
+        sums = [jnp.zeros((1, width), F32)] * 4
+        for block in row_blocks(rows):
+            masked = mask_ref[block] > 0
+            middle = middle_ref[block]
+            back, grad_gain, grad_shift = norm_pull(middle, gain_ref[...], acc_ref[block])
+            grad_middle = jnp.where(masked, cot_ref[block].astype(F32), 0.0) + back
+            gm_ref[block] = grad_middle
+            grad_branch = (s1_ref[...] * grad_middle).astype(BF16)
+            gbr_ref[block] = grad_branch
+            initial = jnp.where(masked, mt_ref[...], tok_ref[block].astype(F32))
+            new = (
+                grad_gain,
+                grad_shift,
+                col_sum(grad_middle * (middle - initial)) / s1_ref[...],
+                col_sum(grad_branch.astype(F32)),
+            )
+            sums = [a + b for a, b in zip(sums, new)]
+        for i, one in enumerate(sums):
+            sums_ref[i : i + 1] = one
+        over = padded(rows) - rows
+        gbr_ref[rows:] = jnp.zeros((over, width), BF16)
+
+
+def back_kernel(
+    rows, me_ref, gbr_ref, wo_ref, ctx_ref, q_ref, k_ref, v_ref, n1_ref,
+    dq_ref, dk_ref, dv_ref, grads_ref, sums_ref, gc_ref,
+):
+    me = me_ref[0]
+    cols = q_ref.shape[1]
+    gc_ref[...] = nt(gbr_ref[...], wo_ref[...]).astype(BF16)
+    factor = 1.0 / math.sqrt(HD)
+    for ref in (dq_ref, dk_ref, dv_ref):
+        ref[padded(rows) - 32 :, :] = jnp.zeros((32, cols), BF16)
+
+    def one_pair(pair, carry):
+        lanes = pl.ds(pl.multiple_of(pair * PAIR, PAIR), PAIR)
+        for start, size, offset in windows(rows):
+            win = slice(start, start + size)
+            q, k, v = q_ref[win, lanes], k_ref[win, lanes], v_ref[win, lanes]
+            keep = inside((size, PAIR), 0, offset)
+            gc = jnp.where(keep, gc_ref[win, lanes], jnp.zeros((size, PAIR), BF16))
+            low_half = lax.broadcasted_iota(jnp.int32, (size, PAIR), 1) < HD
+            here = inside((size, size), 0, offset)
+            got = []
+            for mine in (low_half, ~low_half):
+                zero = jnp.zeros_like(k)
+                k_one = jnp.where(mine, k, zero)
+                scores = jnp.where(here, nt(k_one, q), LOWEST)
+                raised = jnp.exp(scores - jnp.max(scores, axis=0, keepdims=True))
+                probs = raised * (1.0 / jnp.sum(raised, axis=0, keepdims=True))
+                grad_probs = nt(jnp.where(mine, v, zero), gc)
+                inner = jnp.sum(grad_probs * probs, axis=0, keepdims=True)
+                grad_scores = (probs * (grad_probs - inner)).astype(BF16)
+                got.append((tn(grad_scores, k_one), nn(grad_scores, q), nn(probs.astype(BF16), gc)))
+            low, high = got
+            for ref, new in (
+                (dq_ref, (low[0] + high[0]) * factor),
+                (dk_ref, jnp.where(low_half, low[1], high[1])),
+                (dv_ref, jnp.where(low_half, low[2], high[2])),
+            ):
+                ref[win, lanes] = jnp.where(keep, new.astype(BF16), ref[win, lanes])
+        return carry
+
+    lax.fori_loop(0, cols // PAIR, one_pair, 0)
+    for i, ref in enumerate((dq_ref, dk_ref, dv_ref)):
+        store_blocks(me, tn(n1_ref[...], ref[...]), grads_ref, i * cols)
+        if i != 1:
+            sums_ref[i // 2 : i // 2 + 1] = col_sum(ref[...].astype(F32))
+    store_blocks(me, tn(gbr_ref[...], ctx_ref[...]), grads_ref, 3 * cols)
+
+
+def input_kernel(
+    rows, *refs
+):
+    grads, weights = refs[:6], refs[6:12]
+    tok_ref, mask_ref, mt_ref, gain_ref, gm_ref, out_ref, sums_ref = refs[12:]
+    width = out_ref.shape[1]
+    sums = [jnp.zeros((1, width), F32)] * 3
+    for block in row_blocks(rows):
+        grad_normed = None
+        for grad_ref, w_ref in zip(grads, weights):
+            one = nt(grad_ref[block], w_ref[...])
+            grad_normed = one if grad_normed is None else grad_normed + one
+        masked = mask_ref[block] > 0
+        initial = jnp.where(masked, mt_ref[...], tok_ref[block].astype(F32))
+        back, grad_gain, grad_shift = norm_pull(initial, gain_ref[...], grad_normed)
+        grad_initial = gm_ref[block] + back
+        out_ref[block] = jnp.where(masked, 0.0, grad_initial)
+        new = (col_sum(jnp.where(masked, grad_initial, 0.0)), grad_gain, grad_shift)
+        sums = [a + b for a, b in zip(sums, new)]
+    for i, one in enumerate(sums):
+        sums_ref[i : i + 1] = one
+
+
+def output_kernel(
+    rows, count, *refs
+):
+    hiddens, wds = refs[:count], refs[count : 2 * count]
+    middle_ref, mask_ref, cot_ref, bd_ref, s2_ref = refs[2 * count : 2 * count + 5]
+    out_ref, sums_ref, acc_ref = refs[2 * count + 5 :]
+    step = pl.program_id(0)
+    part = None
+    for hidden_ref, wd_ref in zip(hiddens, wds):
+        one = nn(hidden_ref[...], wd_ref[...])
+        part = one if part is None else part + one
+
+    @pl.when(step == 0)
+    def first():
+        acc_ref[...] = part
+
+    @pl.when(step > 0)
+    def later():
+        acc_ref[...] += part
+
+    @pl.when(step == pl.num_programs(0) - 1)
+    def last():
+        total = jnp.zeros((1, out_ref.shape[1]), F32)
+        for block in row_blocks(rows):
+            output = acc_ref[block] + bd_ref[...]
+            out_ref[block] = (middle_ref[block] + s2_ref[...] * output).astype(BF16)
+            grad_block = jnp.where(mask_ref[block] > 0, cot_ref[block].astype(F32), 0.0)
+            total += col_sum(grad_block * output)
+        sums_ref[...] = total
+
+
+def shape_of(shape, dtype=BF16):
+    return jax.ShapeDtypeStruct(shape, dtype)
+
+
+def cost(flops, *arrays):
+    moved = sum(a.size * a.dtype.itemsize for a in arrays)
+    return pl.CostEstimate(flops=flops, bytes_accessed=moved, transcendentals=0)
+
+
+def whole_call(kernel, outs, args, flops, scratch=(), name=None, scalars=0):
+    vmem = pl.BlockSpec(memory_space=pltpu.VMEM)
+    smem = pl.BlockSpec(memory_space=pltpu.SMEM)
+    return pl.pallas_call(
+        kernel,
+        in_specs=[smem] * scalars + [vmem] * (len(args) - scalars),
+        out_specs=[vmem] * len(outs),
+        out_shape=outs,
+        scratch_shapes=list(scratch),
+        compiler_params=pltpu.CompilerParams(vmem_limit_bytes=56 * MIB),
+        cost_estimate=cost(flops, *args, *outs),
+        name=name,
+    )(*args)
+
+
+def feed(me, n2, go, w_up, w_down, b_up, first, count, chunk, n):
+    tall, width = n2.shape
+    cols = count * chunk
+    outs = [
+        shape_of((tall, cols)),
+        shape_of((tall, cols)),
+        shape_of((n, width // n, cols)),
+        shape_of((n, width // n, cols)),
+        shape_of((1, cols), F32),
+    ]
+
+    def all_of(array):
+        return pl.BlockSpec(array.shape, lambda c, me: (0, 0))
+
+    def along(size, base):
+        return pl.BlockSpec((size, chunk), lambda c, me: (0, c + base))
+
+    blocks = pl.BlockSpec((n, width // n, chunk), lambda c, me: (0, 0, c))
+    return pl.pallas_call(
+        feed_kernel,
+        grid_spec=pltpu.PrefetchScalarGridSpec(
+            num_scalar_prefetch=1,
+            grid=(count,),
+            in_specs=[
+                all_of(n2),
+                all_of(go),
+                along(width, first),
+                pl.BlockSpec((chunk, width), lambda c, me: (c + first, 0)),
+                along(1, first),
+            ],
+            out_specs=[along(tall, 0), along(tall, 0), blocks, blocks, along(1, 0)],
+        ),
+        out_shape=outs,
+        compiler_params=pltpu.CompilerParams(vmem_limit_bytes=56 * MIB),
+        cost_estimate=cost(8 * tall * width * cols, n2, go, *outs),
+        name="feed",
+    )(me, n2, go, w_up, w_down, b_up)
+
+
+def summed(kernel, lefts, rights, picks, rights_axis, others, outs, steps, chunk, name):
+    tall = lefts[0].shape[0]
+    width = rights[0].shape[1 - rights_axis]
+    specs = [pl.BlockSpec((tall, chunk), lambda c: (0, c)) for _ in lefts]
+    for base in picks:
+        if rights_axis:
+            specs.append(pl.BlockSpec((width, chunk), lambda c, base=base: (0, c + base)))
+        else:
+            specs.append(pl.BlockSpec((chunk, width), lambda c, base=base: (c + base, 0)))
+    specs += [pl.BlockSpec(a.shape, lambda c: (0, 0)) for a in others]
+    return pl.pallas_call(
+        kernel,
+        grid=(steps,),
+        in_specs=specs,
+        out_specs=[pl.BlockSpec(o.shape, lambda c: (0, 0)) for o in outs],
+        out_shape=outs,
+        scratch_shapes=[pltpu.VMEM((tall, width), F32)],
+        compiler_params=pltpu.CompilerParams(vmem_limit_bytes=56 * MIB),
+        cost_estimate=cost(2 * tall * width * chunk * steps * len(lefts), *lefts, *others, *outs),
+        name=name,
+    )(*lefts, *rights, *others)
+
+
+def pairs(n, bit):
+    return [(i, i ^ (1 << bit)) for i in range(n)]
+
+
+class Scatter:
+    def __init__(self, sources, order):
+        self.n, self.rows, self.cols = sources[0].shape
+        self.order = order
+        self.left = list(range(self.n.bit_length() - 1))[::-1]
+        dims = (2,) * len(self.left) + (self.rows, self.cols)
+        self.sources = [s.reshape(dims) for s in sources]
+
+    def total(self, bit, side):
+        at = self.left.index(bit)
+        parts = [lax.index_in_dim(s, side, at, keepdims=False) for s in self.sources]
+        return parts
+
+    def hop(self, j):
+        bit = self.order[j]
+        send = functools.reduce(jnp.add, [p.astype(F32) for p in self.total(bit, 1)]).astype(BF16)
+        got = lax.ppermute(send, "dp", pairs(self.n, bit))
+        self.sources = self.total(bit, 0) + [got]
+        self.left.remove(bit)
+
+    def result(self):
+        return functools.reduce(jnp.add, [s.astype(F32) for s in self.sources])
+
+
+def swap(array):
+    return lax.ppermute(array, "tp", [(0, 1), (1, 0)])
+
+
+def local_body(
+    tokens, masked, cotangent, mask_token, gain_one, shift_one, w_query, w_key, w_value, b_query,
+    b_value, w_out, b_out, scale_one, gain_two, shift_two, w_up, b_up, w_down, b_down, scale_two,
+):
+    rows, width = tokens.shape
+    tall = padded(rows)
+    half = w_query.shape[1]
+    units = w_up.shape[1]
+    n = lax.axis_size("dp")
+    bits = n.bit_length() - 1
+    me = lax.axis_index("dp").astype(jnp.int32).reshape(1)
+    biases = jnp.concatenate([b_query, b_value, b_up]).reshape(-1, 128)
+
+    wq2, wk2, wv2 = swap(w_query), swap(w_key), swap(w_value)
+    biases2 = swap(biases).reshape(-1)
+    wo2 = swap(w_out)
+    wu2, wd2 = swap(w_up), swap(w_down)
+    row = lambda v: v.reshape(1, -1)
+    bq2, bv2, bu2 = row(biases2[:half]), row(biases2[half : 2 * half]), row(biases2[2 * half :])
+    bq, bv, bu = row(b_query), row(b_value), row(b_up)
+    mt, g1, s1, bo, sc1 = row(mask_token), row(gain_one), row(shift_one), row(b_out), row(scale_one)
+    g2, s2, bd, sc2 = row(gain_two), row(shift_two), row(b_down), row(scale_two)
+    mask = masked.reshape(rows, 1)
+
+    narrow = shape_of((tall, half))
+    wide = shape_of((tall, width))
+    attend_flops = 2 * 2 * 256 * SEQ * rows * half // HD
+    normed, q, k, v, ctx = whole_call(
+        functools.partial(first_kernel, rows),
+        [wide, narrow, narrow, narrow, narrow],
+        (tokens, mask, mt, g1, s1, w_query, w_key, w_value, bq, bv),
+        6 * rows * width * half + attend_flops,
+        name="first",
+    )
+    q2, k2, v2, ctx2, middle, normed2, go, sum_go = whole_call(
+        functools.partial(second_kernel, rows),
+        [narrow, narrow, narrow, narrow, shape_of((rows, width), F32), wide, wide, shape_of((1, width), F32)],
+        (normed, wq2, wk2, wv2, bq2, bv2, ctx, w_out, wo2, bo, sc1, g2, s2, tokens, mask, mt, cotangent, sc2),
+        10 * rows * width * half + attend_flops,
+        name="second",
+    )
+
+    chunk = min(512, units)
+    steps = units // chunk
+    cuts = 2 if steps % 2 == 0 else 1
+    per = steps // cuts
+    hiddens, gps, firsts, grads, sums_up, sums_up2 = [], [], [], [], [], []
+    for cut in range(cuts):
+        his = feed(me, normed2, go, wu2, wd2, bu2, cut * per, per, chunk, n)
+        theirs = (swap(his[2]), swap(his[3]))
+        own = feed(me, normed2, go, w_up, w_down, bu, cut * per, per, chunk, n)
+        grads.append(((own[2], theirs[0]), (own[3], theirs[1])))
+        hiddens += [his[0], own[0]]
+        gps += [his[1], own[1]]
+        sums_up2.append(his[4])
+        sums_up.append(own[4])
+        firsts += [cut * per] * 2
+    ups, downs = [wu2, w_up] * cuts, [wd2, w_down] * cuts
+
+    gm, gbr, sums_two = summed(
+        functools.partial(middle_kernel, rows, len(gps)),
+        gps, ups, firsts, 1,
+        (middle, tokens, mask, mt, cotangent, g2, sc1),
+        [shape_of((rows, width), F32), wide, shape_of((4, width), F32)],
+        per, chunk, "middle",
+    )
+
+    def back(wo, ctx, q, k, v):
+        return pl_back(rows, me, gbr, wo, ctx, q, k, v, normed, n, attend_flops)
+
+    dq2, dk2, dv2, gw2, sums_b2 = back(wo2, ctx2, q2, k2, v2)
+    gw2 = swap(gw2)
+    dq, dk, dv, gw, sums_b = back(w_out, ctx, q, k, v)
+
+    grad_tokens, sums_one = whole_call(
+        functools.partial(input_kernel, rows),
+        [shape_of((rows, width), F32), shape_of((3, width), F32)],
+        (dq, dk, dv, dq2, dk2, dv2, w_query, w_key, w_value, wq2, wk2, wv2, tokens, mask, mt, g1, gm),
+        12 * rows * width * half,
+        name="input",
+    )
+    block_out, sum_two = summed(
+        functools.partial(output_kernel, rows, len(hiddens)),
+        hiddens, downs, firsts, 0,
+        (middle, mask, cotangent, bd, sc2),
+        [shape_of((rows, width)), shape_of((1, width), F32)],
+        per, chunk, "output",
+    )
+
+    natural = tuple(range(bits))
+    orders = [natural[i:] + natural[:i] for i in range(bits)]
+    by_x, by_z = orders[0], orders[2 % bits]
+    by_y = natural[1:2] + natural[0:1] + natural[2:]
+    done = {}
+
+    def part(sources, low, high):
+        return [s[:, :, low:high] for s in sources]
+
+    groups = []
+    for cut, (down, up) in enumerate(grads):
+        cols = down[0].shape[2]
+        at = cols * 3 // 4
+        groups.append([
+            (("down", cut, 0), Scatter(part(down, 0, at), by_x)),
+            (("up", cut, 0), Scatter(part(up, 0, at), by_y)),
+            (("rest", cut, 0), Scatter([jnp.concatenate([d[:, :, at:], u[:, :, at:]], axis=2) for d, u in zip(down, up)], by_z)),
+        ])
+    cols = gw.shape[2]
+    lows = [0, cols * 3 // 8, cols * 3 // 4, cols]
+    groups.append([
+        (("attention", 0, i), Scatter(part((gw, gw2), lows[i], lows[i + 1]), (by_x, by_y, by_z)[i])) for i in range(3)
+    ])
+    for group in groups:
+        for j in range(bits):
+            for _, one in group:
+                one.hop(j)
+        for name, one in group:
+            done[name] = one.result()
+    downs_, ups_ = [], []
+    for cut in range(cuts):
+        rest = done["rest", cut, 0]
+        mid = rest.shape[1] // 2
+        downs_ += [done["down", cut, 0], rest[:, :mid]]
+        ups_ += [done["up", cut, 0], rest[:, mid:]]
+    grad_w_down = jnp.concatenate(downs_, axis=1).T
+    grad_w_up = jnp.concatenate(ups_, axis=1)
+    attention = jnp.concatenate([done["attention", 0, i] for i in range(3)], axis=1)
+
+    same = jnp.concatenate([sums_one.reshape(-1), sums_two.reshape(-1), sum_go.reshape(-1), sum_two.reshape(-1)])
+    own_sums = jnp.concatenate([sums_b.reshape(-1)] + [s.reshape(-1) for s in sums_up])
+    other_sums = jnp.concatenate([sums_b2.reshape(-1)] + [s.reshape(-1) for s in sums_up2])
+    vector = jnp.concatenate([same, own_sums]).reshape(-1, 128)
+    vector += swap(jnp.concatenate([same, other_sums]).reshape(-1, 128))
+    for bit in range(bits):
+        vector += lax.ppermute(vector, "dp", pairs(n, bit))
+    vector = vector.reshape(-1)
+    rep = [vector[i * width : (i + 1) * width] for i in range(9)]
+    (grad_mask_token, grad_gain_one, grad_shift_one, grad_gain_two, grad_shift_two, grad_scale_one,
+     grad_b_out, grad_b_down, grad_scale_two) = rep
+    own = vector[9 * width :]
+    return (
+        block_out,
+        grad_tokens,
+        grad_mask_token,
+        grad_gain_one,
+        grad_shift_one,
+        attention[:, :half],
+        attention[:, half : 2 * half],
+        attention[:, 2 * half : 3 * half],
+        own[:half],
+        own[half : 2 * half],
+        attention[:, 3 * half :].T,
+        grad_b_out,
+        grad_scale_one,
+        grad_gain_two,
+        grad_shift_two,
+        grad_w_up,
+        own[2 * half :],
+        grad_w_down,
+        grad_b_down,
+        grad_scale_two,
+    )
+
+
+def pl_back(rows, me, gbr, wo, ctx, q, k, v, normed, n, attend_flops):
+    tall, cols = q.shape
+    width = gbr.shape[1]
+    narrow = shape_of((tall, cols))
+    return whole_call(
+        functools.partial(back_kernel, rows),
+        [narrow, narrow, narrow, shape_of((n, width // n, 4 * cols)), shape_of((2, cols), F32)],
+        (me, gbr, wo, ctx, q, k, v, normed),
+        10 * rows * width * cols + 3 * attend_flops,
+        scratch=[pltpu.VMEM((tall, cols), BF16)],
+        name="back",
+        scalars=1,
+    )
+
+
 def solution(mesh):
     placed = (
         P(("dp", "tp"), None),
@@ -285,8 +903,9 @@
         P(),
         P(),
     )
+    fits = mesh.shape["tp"] == 2 and mesh.shape["dp"].bit_count() == 1
     return jax.shard_map(
-        body,
+        local_body if fits else gathered_body,
         mesh=mesh,
         in_specs=placed,
         out_specs=(

time: 692 us -> 400 us (0.58)
  Pallas kernels: 0 us -> 188 us
  matrix products: 171 us -> 0 us
  blocking collectives: 146 us -> 0 us
  local copies, waits for them, and re-layouts: 145 us -> 19.5 us
  other arithmetic: 79.4 us -> 8.98 us
  starting transfers between devices: 8.21 us -> 54.5 us
  between operations: 15.8 us -> 2.13 us
    pallas_call x0 -> x11, Pallas kernels: none -> 188 us  [the longest x5 97.3 us: whole_call(): pl.pallas_call(kernel, in_specs=[smem] * scalars + [vmem] * (len(args) -...]
    dot_general x18 -> x0, matrix products: 171 us -> none  [the longest x4 59.2 us: times_transposed(): lax.dot_general(left, right, (((1,), (1,)), ((), ())), preferred_element_...]
    ppermute x0 -> x53, waiting for transfers between devices: none -> 123 us  [the longest x36 108 us: hop(): got = lax.ppermute(send, 'dp', pairs(self.n, bit))]
    psum x2 -> x0, blocking collectives: 118 us -> none  [the longest x1 77.9 us: body(): lax.psum((grad_b_query, grad_b_value, grad_b_up), 'dp')]
    reduce_scatter x4 -> x0, waiting for transfers between devices: 102 us -> none  [the longest x1 102 us: body(): lax.psum_scatter(grad_w_joined.astype(jnp.bfloat16), 'dp', scatter_dimens...]
    unnamed x139 -> x53, local copies, waits for them, and re-layouts: 76.5 us -> 4.23 us
    ppermute x0 -> x53, starting transfers between devices: none -> 54.5 us  [the longest x36 40.6 us: hop(): got = lax.ppermute(send, 'dp', pairs(self.n, bit))]
    reshape x11 -> x2, local copies, waits for them, and re-layouts: 50.5 us -> 2.36 us  [the longest x1 1.63 us: local_body(): mask = masked.reshape(rows, 1)]
  transfers between devices with their start and end apart: 12 -> 53, of which waited for: 5 -> 30; matrix products, arithmetic and copies ran while one was open for 44% -> 6% of each run, Pallas kernels for 0% -> 44%
where the time goes in v1:
time: 400 us; the launch traced here: 396 us
  Pallas kernels  188 us (47%)
  waiting for transfers between devices  123 us (31%)
  starting transfers between devices  54.5 us (14%)
  local copies, waits for them, and re-layouts  19.5 us (5%)
  other arithmetic  8.98 us (2%)
    ppermute x36, waiting for transfers between devices, hop(): got = lax.ppermute(send, 'dp', pairs(self.n, bit))  108 us
    pallas_call x5, Pallas kernels, whole_call(): pl.pallas_call(kernel, in_specs=[smem] * scalars + [vmem] * (len(args) -...  97.3 us
    pallas_call x4, Pallas kernels, feed(): pl.pallas_call(feed_kernel, grid_spec=pltpu.PrefetchScalarGridSpec(num_sc...  54.9 us
    ppermute x36, starting transfers between devices, hop(): got = lax.ppermute(send, 'dp', pairs(self.n, bit))  40.6 us
    pallas_call x2, Pallas kernels, summed(): pl.pallas_call(kernel, grid=(steps,), in_specs=specs, out_specs=[pl.Block...  35.7 us
    ppermute x4, starting transfers between devices, local_body(): vector += lax.ppermute(vector, 'dp', pairs(n, bit))  10.6 us
    ppermute x13, waiting for transfers between devices, swap(): return lax.ppermute(array, 'tp', [(0, 1), (1, 0)])  8.19 us
  transfers between devices with their start and end apart: 53, of which 30 were waited for; matrix products, arithmetic and copies ran while one was open for 6% of the time, Pallas kernels for 44%

profile of v1, /device:TPU:0, one launch (start us, length us, event | category | flops | bytes accessed | tf_op | source)
XLA Modules:
  0.0 396.4 jit_solution(8812438707167494694)
XLA Ops:
  2.9 6.0 %collective-permute-done.3 = f32[24,128]{1,0:T(8,128)S(1)} collective-permute-done((f32[24,128]{1,0:T(8,128)S(1)}, f32[24,128]{1,0:T(8,128)S(1)}, u32[]{:S(2)}, u32[]{:S(2)}) %collective-permute-start.3) | collective-permute-done | bytes 12320 | tf_op jit(solution)/shard_map/ppermute | solution.py:700
  9.3 1.2 collective-permute-done.wq_ref.refs_9_
  10.7 1.6 reshape.763.mask_ref.refs_9_.refs_10_.refs_13_
  12.3 12.6 %first.1 = (bf16[800,1024]{1,0:T(8,128)(2,1)}, bf16[800,512]{1,0:T(8,128)(2,1)}, bf16[800,512]{1,0:T(8,128)(2,1)}, bf16[800,512]{1,0:T(8,128)(2,1)}, bf16[800,512]{1,0:T(8,128)(2,1)}) custom-call(bf16[788,1024]{1,0:T(8,128)(2,1)} %refs_12_.3, s32[788,1]{1,0:T(8,128)} %reshape.763.mask_ref.refs_9_.refs_10_.refs_13_, f32[1,1024]{1,0:T(1,128)} %bitcast.469, ...), custom_call_target="tpu_custom_call" | custom-call | flops 3750526976 | bytes 9694288 | tf_op jit(solution)/shard_map/first/pallas_call | solution.py:597
  27.5 17.8 %second.1 = (bf16[800,512]{1,0:T(8,128)(2,1)}, bf16[800,512]{1,0:T(8,128)(2,1)}, bf16[800,512]{1,0:T(8,128)(2,1)}, bf16[800,512]{1,0:T(8,128)(2,1)}, f32[788,102...) custom-call(bf16[800,1024]{1,0:T(8,128)(2,1)} %get-tuple-element.70.normed_ref.n1_ref, ...), custom_call_target="tpu_custom_call" | custom-call | flops 5403082752 | bytes 20745296 | tf_op jit(solution)/shard_map/second/pallas_call | solution.py:597
  45.3 13.5 %feed.7 = (bf16[800,1024]{1,0:T(8,128)(2,1)}, bf16[800,1024]{1,0:T(8,128)(2,1)}, bf16[16,64,1024]{2,1,0:T(8,128)(2,1)}, bf16[16,64,1024]{2,1,0:T(8,128)(2,1)}, f32[1,1024]{1,0:T(1,128)}) custom-call(s32[1]{0:T(128)} %bitcast.me_ref, bf16[800,1024]{1,0:T(8,128)(2,1)} %get-tuple-element.72.n2_ref, bf16[800,1024]{1,0:T(8,128)(2,1)} %get-tuple-element.73.go_ref, ...), custom_call_target="tpu_custom_call" | custom-call | flops 6710886400 | bytes 10752000 | tf_op jit(solution)/shard_map/feed/pallas_call | solution.py:627
  58.8 14.1 %feed.5 = (bf16[800,1024]{1,0:T(8,128)(2,1)}, bf16[800,1024]{1,0:T(8,128)(2,1)}, bf16[16,64,1024]{2,1,0:T(8,128)(2,1)}, bf16[16,64,1024]{2,1,0:T(8,128)(2,1)}, f32[1,1024]{1,0:T(1,128)}) custom-call(s32[1]{0:T(128)} %bitcast.me_ref, bf16[800,1024]{1,0:T(8,128)(2,1)} %get-tuple-element.72.n2_ref, bf16[800,1024]{1,0:T(8,128)(2,1)} %get-tuple-element.73.go_ref, ...), custom_call_target="tpu_custom_call" | custom-call | flops 6710886400 | bytes 10752000 | tf_op jit(solution)/shard_map/feed/pallas_call | solution.py:627
  72.9 13.5 %feed.6 = (bf16[800,1024]{1,0:T(8,128)(2,1)}, bf16[800,1024]{1,0:T(8,128)(2,1)}, bf16[16,64,1024]{2,1,0:T(8,128)(2,1)}, bf16[16,64,1024]{2,1,0:T(8,128)(2,1)}, f32[1,1024]{1,0:T(1,128)}) custom-call(s32[1]{0:T(128)} %bitcast.me_ref, bf16[800,1024]{1,0:T(8,128)(2,1)} %get-tuple-element.72.n2_ref, bf16[800,1024]{1,0:T(8,128)(2,1)} %get-tuple-element.73.go_ref, ...), custom_call_target="tpu_custom_call" | custom-call | flops 6710886400 | bytes 10752000 | tf_op jit(solution)/shard_map/feed/pallas_call | solution.py:627
  87.0 13.8 %feed.4 = (bf16[800,1024]{1,0:T(8,128)(2,1)}, bf16[800,1024]{1,0:T(8,128)(2,1)}, bf16[16,64,1024]{2,1,0:T(8,128)(2,1)}, bf16[16,64,1024]{2,1,0:T(8,128)(2,1)}, f32[1,1024]{1,0:T(1,128)}) custom-call(s32[1]{0:T(128)} %bitcast.me_ref, bf16[800,1024]{1,0:T(8,128)(2,1)} %get-tuple-element.72.n2_ref, bf16[800,1024]{1,0:T(8,128)(2,1)} %get-tuple-element.73.go_ref, ...), custom_call_target="tpu_custom_call" | custom-call | flops 6710886400 | bytes 10752000 | tf_op jit(solution)/shard_map/feed/pallas_call | solution.py:627
  101.0 20.1 %middle.1 = (f32[788,1024]{1,0:T(8,128)}, bf16[800,1024]{1,0:T(8,128)(2,1)}, f32[4,1024]{1,0:T(4,128)}) custom-call(bf16[800,1024]{1,0:T(8,128)(2,1)} %get-tuple-element.80.refs_0_, bf16[800,1024]{1,0:T(8,128)(2,1)} %get-tuple-element.81.refs_1_, bf16[800,1024]{1,0:T(8,128)(2,1)} %get-tuple-element.82.refs_2_, bf16[800,1024]{1,0:T(8,128)(2,1)} %get-tuple-element.83.refs_3_, ...), custom_call_target="tpu_custom_call" | custom-call | flops 6710886400 | bytes 17906768 | tf_op jit(solution)/shard_map/middle/pallas_call | solution.py:658
  121.2 23.9 %back.3 = (bf16[800,512]{1,0:T(8,128)(2,1)}, bf16[800,512]{1,0:T(8,128)(2,1)}, bf16[800,512]{1,0:T(8,128)(2,1)}, bf16[16,64,2048]{2,1,0:T(8,128)(2,1)}, f32[2,512]{1,0:T(2,128)}) custom-call(s32[1]{0:T(128)} %bitcast.me_ref, bf16[800,1024]{1,0:T(8,128)(2,1)} %get-tuple-element.84.gbr_ref, bf16[512,1024]{1,0:T(8,128)(2,1)} %collective-permute-done.4.wo2_ref.wo_ref, ...), custom_call_target="tpu_custom_call" | custom-call | flops 7946469376 | bytes 14258180 | tf_op jit(solution)/shard_map/back/pallas_call | solution.py:597
  145.8 24.0 %back.2 = (bf16[800,512]{1,0:T(8,128)(2,1)}, bf16[800,512]{1,0:T(8,128)(2,1)}, bf16[800,512]{1,0:T(8,128)(2,1)}, bf16[16,64,2048]{2,1,0:T(8,128)(2,1)}, f32[2,512]{1,0:T(2,128)}) custom-call(s32[1]{0:T(128)} %bitcast.me_ref, bf16[800,1024]{1,0:T(8,128)(2,1)} %get-tuple-element.84.gbr_ref, bf16[512,1024]{1,0:T(8,128)(2,1)} %wo_ref.3, ...), custom_call_target="tpu_custom_call" | custom-call | flops 7946469376 | bytes 14258180 | tf_op jit(solution)/shard_map/back/pallas_call | solution.py:597
  170.5 18.9 %input.1 = (f32[788,1024]{1,0:T(8,128)}, f32[3,1024]{1,0:T(4,128)}) custom-call(bf16[800,512]{1,0:T(8,128)(2,1)} %get-tuple-element.88.refs_0_, bf16[800,512]{1,0:T(8,128)(2,1)} %get-tuple-element.89.refs_1_, bf16[800,512]{1,0:T(8,128)(2,1)} %get-tuple-element.90.refs_2_, bf16[800,512]{1,0:T(8,128)(2,1)} %get-tuple-element.95.refs_3_, ...), custom_call_target="tpu_custom_call" | custom-call | flops 4957667328 | bytes 19299408 | tf_op jit(solution)/shard_map/input/pallas_call | solution.py:597
  190.2 15.6 %output.1 = (bf16[788,1024]{1,0:T(8,128)(2,1)}, f32[1,1024]{1,0:T(1,128)}) custom-call(bf16[800,1024]{1,0:T(8,128)(2,1)} %get-tuple-element.74.refs_0_, bf16[800,1024]{1,0:T(8,128)(2,1)} %get-tuple-element.75.refs_1_, bf16[800,1024]{1,0:T(8,128)(2,1)} %get-tuple-element.76.refs_2_, bf16[800,1024]{1,0:T(8,128)(2,1)} %get-tuple-element.77.refs_3_, ...), custom_call_target="tpu_custom_call" | custom-call | flops 6710886400 | bytes 13024336 | tf_op jit(solution)/shard_map/output/pallas_call | solution.py:658
  207.9 3.1 collective-permute-start.8
  211.3 1.9 collective-permute-done.8
  213.3 1.9 collective-permute-start.9
  215.5 1.9 collective-permute-done.9
  217.5 2.0 collective-permute-start.10
  220.2 1.4 collective-permute-done.10
  221.6 3.5 collective-permute-start.11
  225.6 1.5 collective-permute-done.11
  232.1 1.5 slice.1422
  234.3 1.6 collective-permute-start.36
  235.9 1.5 slice.1499
  237.8 1.4 collective-permute-start.41
  239.4 1.6 collective-permute-start.49
  243.4 9.2 %collective-permute-done.41 = bf16[2,2,2,64,512]{4,3,2,1,0:T(8,128)(2,1)S(1)} collective-permute-done((bf16[2,2,2,64,512]{4,3,2,1,0:T(8,128)(2,1)S(1)}, bf16[2,2,2,64,512]{4,3,2,1,0:T(8,128)(2,1)S(1)}, u32[]{:S(2)}, u32[]{:S(2)}) %collective-permute-start.41) | collective-permute-done | bytes 524320 | tf_op jit(solution)/shard_map/ppermute | solution.py:691
  253.2 9.9 %collective-permute-done.31 = bf16[2,2,2,64,512]{4,3,2,1,0:T(8,128)(2,1)S(1)} collective-permute-done((bf16[2,2,2,64,512]{4,3,2,1,0:T(8,128)(2,1)S(1)}, bf16[2,2,2,64,512]{4,3,2,1,0:T(8,128)(2,1)S(1)}, u32[]{:S(2)}, u32[]{:S(2)}) %collective-permute-start.31) | collective-permute-done | bytes 524320 | tf_op jit(solution)/shard_map/ppermute | solution.py:691
  263.1 1.5 collective-permute-start.45
  264.8 3.0 collective-permute-start.42
  267.9 11.0 %collective-permute-done.42 = bf16[2,2,64,512]{3,2,1,0:T(8,128)(2,1)S(1)} collective-permute-done((bf16[2,2,64,512]{3,2,1,0:T(8,128)(2,1)S(1)}, bf16[2,2,64,512]{3,2,1,0:T(8,128)(2,1)S(1)}, u32[]{:S(2)}, u32[]{:S(2)}) %collective-permute-start.42) | collective-permute-done | bytes 262176 | tf_op jit(solution)/shard_map/ppermute | solution.py:691
  279.7 13.0 %collective-permute-done.32 = bf16[2,2,64,512]{3,2,1,0:T(8,128)(2,1)S(1)} collective-permute-done((bf16[2,2,64,512]{3,2,1,0:T(8,128)(2,1)S(1)}, bf16[2,2,64,512]{3,2,1,0:T(8,128)(2,1)S(1)}, u32[]{:S(2)}, u32[]{:S(2)}) %collective-permute-start.32) | collective-permute-done | bytes 262176 | tf_op jit(solution)/shard_map/ppermute | solution.py:691
  294.2 1.6 collective-permute-start.33
  296.0 2.2 collective-permute-done.43
  298.1 1.4 collective-permute-start.27
  299.6 1.3 collective-permute-done.33
  300.9 1.4 collective-permute-start.44
  302.4 2.8 collective-permute-done.44
  305.2 1.4 collective-permute-start.34
  306.7 3.6 collective-permute-done.34
  310.2 1.4 collective-permute-start.46
  312.1 2.1 collective-permute-start.51
  314.3 3.7 collective-permute-done.46
  318.2 2.4 collective-permute-done.38
  321.0 4.0 collective-permute-done.51
  325.5 2.7 collective-permute-done.28
  328.2 1.2 collective-permute-start.29
  329.4 2.2 collective-permute-done.47
  331.8 3.7 collective-permute-done.52
  335.7 2.0 collective-permute-done.29
  341.5 1.5 collective-permute-start.13
  343.2 1.2 collective-permute-start.17
  344.5 7.1 %collective-permute-done.21 = bf16[2,2,2,64,512]{4,3,2,1,0:T(8,128)(2,1)S(1)} collective-permute-done((bf16[2,2,2,64,512]{4,3,2,1,0:T(8,128)(2,1)S(1)}, bf16[2,2,2,64,512]{4,3,2,1,0:T(8,128)(2,1)S(1)}, u32[]{:S(2)}, u32[]{:S(2)}) %collective-permute-start.21) | collective-permute-done | bytes 524320 | tf_op jit(solution)/shard_map/ppermute | solution.py:691
  351.7 2.7 collective-permute-start.22
  354.4 9.5 %collective-permute-done.22 = bf16[2,2,64,512]{3,2,1,0:T(8,128)(2,1)S(1)} collective-permute-done((bf16[2,2,64,512]{3,2,1,0:T(8,128)(2,1)S(1)}, bf16[2,2,64,512]{3,2,1,0:T(8,128)(2,1)S(1)}, u32[]{:S(2)}, u32[]{:S(2)}) %collective-permute-start.22) | collective-permute-done | bytes 262176 | tf_op jit(solution)/shard_map/ppermute | solution.py:691
  364.0 1.4 collective-permute-start.23
  365.5 1.5 collective-permute-start.14
  367.3 2.9 collective-permute-done.23
  370.8 5.9 %collective-permute-done.24 = bf16[64,512]{1,0:T(8,128)(2,1)S(1)} collective-permute-done((bf16[64,512]{1,0:T(8,128)(2,1)S(1)}, bf16[64,512]{1,0:T(8,128)(2,1)S(1)}, u32[]{:S(2)}, u32[]{:S(2)}) %collective-permute-start.24) | collective-permute-done | bytes 65568 | tf_op jit(solution)/shard_map/ppermute | solution.py:691
  379.8 5.6 %collective-permute-done.15 = bf16[2,64,768]{2,1,0:T(8,128)(2,1)S(1)} collective-permute-done((bf16[2,64,768]{2,1,0:T(8,128)(2,1)S(1)}, bf16[2,64,768]{2,1,0:T(8,128)(2,1)S(1)}, u32[]{:S(2)}, u32[]{:S(2)}) %collective-permute-start.15) | collective-permute-done | bytes 196640 | tf_op jit(solution)/shard_map/ppermute | solution.py:691
  385.5 2.5 collective-permute-start.16
  388.0 3.5 collective-permute-start.20
  392.5 2.6 collective-permute-done.20
  (225 shorter events, 36.1 us)
Async XLA Ops:
  0.7 72.3 %collective-permute-start.5 = (bf16[1024,2048]{1,0:T(8,128)(2,1)}, bf16[1024,2048]{1,0:T(8,128)(2,1)}, u32[]{:S(2)}, u32[]{:S(2)}) collective-permute-start(bf16[1024,2048]{1,0:T(8,128)(2,1)} %refs_7_.4), channel_id=1, source_target_pairs={{0,1},{1,0},{2,3},{3,2},{4,5},{5,4},{6,7},{7,6},{8,9},{9,8},{10,11... | collective-permute-start | bytes 12582920 | tf_op jit(solution)/shard_map/ppermute | solution.py:700
  1.2 71.8 %collective-permute-start.6 = (bf16[2048,1024]{1,0:T(8,128)(2,1)}, bf16[2048,1024]{1,0:T(8,128)(2,1)}, u32[]{:S(2)}, u32[]{:S(2)}) collective-permute-start(bf16[2048,1024]{1,0:T(8,128)(2,1)} %refs_7_.3), channel_id=1, source_target_pairs={{0,1},{1,0},{2,3},{3,2},{4,5},{5,4},{6,7},{7,6},{8,9},{9,8},{10,11... | collective-permute-start | bytes 12582920 | tf_op jit(solution)/shard_map/ppermute | solution.py:700
  1.3 9.2 %collective-permute-start = (bf16[1024,512]{1,0:T(8,128)(2,1)}, bf16[1024,512]{1,0:T(8,128)(2,1)S(1)}, u32[]{:S(2)}, u32[]{:S(2)}) collective-permute-start(bf16[1024,512]{1,0:T(8,128)(2,1)} %refs_6_.1), channel_id=1, source_target_pairs={{0,1},{1,0},{2,3},{3,2},{4,5},{5,4},{6,7},{7,6},{8,9},{9,8},{10,11... | collective-permute-start | bytes 3145736 | tf_op jit(solution)/shard_map/ppermute | solution.py:700
  2.4 6.5 %collective-permute-start.3 = (f32[24,128]{1,0:T(8,128)S(1)}, f32[24,128]{1,0:T(8,128)S(1)}, u32[]{:S(2)}, u32[]{:S(2)}) collective-permute-start(f32[24,128]{1,0:T(8,128)S(1)} %maximum_bitcast_fusion.1), channel_id=1, source_target_pairs={{0,1},{1,0},{2,3},{3,2},{4,5},{5,4},{6,7},{7,6},{8,9},{9,8},{10,11... | collective-permute-start | bytes 36872 | tf_op jit(solution)/shard_map/ppermute | solution.py:700
  2.5 23.7 %collective-permute-start.1 = (bf16[1024,512]{1,0:T(8,128)(2,1)}, bf16[1024,512]{1,0:T(8,128)(2,1)S(1)}, u32[]{:S(2)}, u32[]{:S(2)}) collective-permute-start(bf16[1024,512]{1,0:T(8,128)(2,1)} %refs_7_.5), channel_id=1, source_target_pairs={{0,1},{1,0},{2,3},{3,2},{4,5},{5,4},{6,7},{7,6},{8,9},{9,8},{10,11... | collective-permute-start | bytes 3145736 | tf_op jit(solution)/shard_map/ppermute | solution.py:700
  8.9 17.2 %collective-permute-start.2 = (bf16[1024,512]{1,0:T(8,128)(2,1)}, bf16[1024,512]{1,0:T(8,128)(2,1)S(1)}, u32[]{:S(2)}, u32[]{:S(2)}) collective-permute-start(bf16[1024,512]{1,0:T(8,128)(2,1)} %refs_8_.1), channel_id=1, source_target_pairs={{0,1},{1,0},{2,3},{3,2},{4,5},{5,4},{6,7},{7,6},{8,9},{9,8},{10,11... | collective-permute-start | bytes 3145736 | tf_op jit(solution)/shard_map/ppermute | solution.py:700
  10.5 14.5 %copy-start.12 = (bf16[1024,512]{1,0:T(8,128)(2,1)}, bf16[1024,512]{1,0:T(8,128)(2,1)S(1)}, u32[]{:S(2)}) copy-start(bf16[1024,512]{1,0:T(8,128)(2,1)S(1)} %collective-permute-done.wq_ref.refs_9_) | copy-start | bytes 3145732
  10.5 15.7 %collective-permute-start.4 = (bf16[512,1024]{1,0:T(8,128)(2,1)}, bf16[512,1024]{1,0:T(8,128)(2,1)}, u32[]{:S(2)}, u32[]{:S(2)}) collective-permute-start(bf16[512,1024]{1,0:T(8,128)(2,1)} %wo_ref.3), channel_id=1, source_target_pairs={{0,1},{1,0},{2,3},{3,2},{4,5},{5,4},{6,7},{7,6},{8,9},{9,8},{10,11... | collective-permute-start | bytes 3145736 | tf_op jit(solution)/shard_map/ppermute | solution.py:700
  86.4 142.7 %collective-permute-start.35 = (bf16[16,64,1024]{2,1,0:T(8,128)(2,1)}, bf16[16,64,1024]{2,1,0:T(8,128)(2,1)}, u32[]{:S(2)}, u32[]{:S(2)}) collective-permute-start(bf16[16,64,1024]{2,1,0:T(8,128)(2,1)} %get-tuple-element.117), channel_id=1, source_target_pairs={{0,1},{1,0},{2,3},{3,2},{4,5},{5,4},{6,7},{7,6},{8,9},{9,8},{10,11... | collective-permute-start | bytes 6291464 | tf_op jit(solution)/shard_map/ppermute | solution.py:700
  86.7 143.5 %collective-permute-start.40 = (bf16[16,64,1024]{2,1,0:T(8,128)(2,1)}, bf16[16,64,1024]{2,1,0:T(8,128)(2,1)}, u32[]{:S(2)}, u32[]{:S(2)}) collective-permute-start(bf16[16,64,1024]{2,1,0:T(8,128)(2,1)} %get-tuple-element.119), channel_id=1, source_target_pairs={{0,1},{1,0},{2,3},{3,2},{4,5},{5,4},{6,7},{7,6},{8,9},{9,8},{10,11... | collective-permute-start | bytes 6291464 | tf_op jit(solution)/shard_map/ppermute | solution.py:700
  100.8 130.6 %collective-permute-start.25 = (bf16[16,64,1024]{2,1,0:T(8,128)(2,1)}, bf16[16,64,1024]{2,1,0:T(8,128)(2,1)S(1)}, u32[]{:S(2)}, u32[]{:S(2)}) collective-permute-start(bf16[16,64,1024]{2,1,0:T(8,128)(2,1)} %get-tuple-element.113), channel_id=1, source_target_pairs={{0,1},{1,0},{2,3},{3,2},{4,5},{5,4},{6,7},{7,6},{8,9},{9,8},{10,11... | collective-permute-start | bytes 6291464 | tf_op jit(solution)/shard_map/ppermute | solution.py:700
  170.5 19.6 %copy-start.5 = (f32[4,1024]{1,0:T(4,128)S(1)}, f32[4,1024]{1,0:T(4,128)}, u32[]{:S(2)}) copy-start(f32[4,1024]{1,0:T(4,128)} %get-tuple-element.101) | copy-start | bytes 49156
  170.5 19.7 %copy-start.8 = (f32[1,1024]{1,0:T(1,128)S(1)}, f32[1,1024]{1,0:T(1,128)}, u32[]{:S(2)}) copy-start(f32[1,1024]{1,0:T(1,128)} %get-tuple-element.102) | copy-start | bytes 12292
  190.1 16.4 %copy-start.10 = (f32[1,1024]{1,0:T(1,128)S(1)}, f32[1,1024]{1,0:T(1,128)}, u32[]{:S(2)}) copy-start(f32[1,1024]{1,0:T(1,128)} %get-tuple-element.108) | copy-start | bytes 12292
  190.2 16.4 %copy-start.9 = (f32[1,1024]{1,0:T(1,128)S(1)}, f32[1,1024]{1,0:T(1,128)}, u32[]{:S(2)}) copy-start(f32[1,1024]{1,0:T(1,128)} %get-tuple-element.109) | copy-start | bytes 12292
  190.2 16.7 %copy-start.7 = (f32[1,1024]{1,0:T(1,128)S(1)}, f32[1,1024]{1,0:T(1,128)}, u32[]{:S(2)}) copy-start(f32[1,1024]{1,0:T(1,128)} %get-tuple-element.105) | copy-start | bytes 12292
  190.2 16.7 %copy-start.6 = (f32[1,1024]{1,0:T(1,128)S(1)}, f32[1,1024]{1,0:T(1,128)}, u32[]{:S(2)}) copy-start(f32[1,1024]{1,0:T(1,128)} %get-tuple-element.106) | copy-start | bytes 12292
  190.2 20.8 %copy-start.2 = (bf16[16,64,1024]{2,1,0:T(8,128)(2,1)S(1)}, bf16[16,64,1024]{2,1,0:T(8,128)(2,1)}, u32[]{:S(2)}) copy-start(bf16[16,64,1024]{2,1,0:T(8,128)(2,1)} %get-tuple-element.116) | copy-start | bytes 6291460
  190.2 20.9 %copy-start.1 = (bf16[16,64,1024]{2,1,0:T(8,128)(2,1)S(1)}, bf16[16,64,1024]{2,1,0:T(8,128)(2,1)}, u32[]{:S(2)}) copy-start(bf16[16,64,1024]{2,1,0:T(8,128)(2,1)} %get-tuple-element.118) | copy-start | bytes 6291460
  206.6 1.3 collective-permute-start.7
  207.9 5.4 %collective-permute-start.8 = (f32[96,128]{1,0:T(8,128)S(1)}, f32[96,128]{1,0:T(8,128)S(1)}, u32[]{:S(2)}, u32[]{:S(2)}) collective-permute-start(f32[96,128]{1,0:T(8,128)S(1)} %bitcast_add_fusion), channel_id=1, source_target_pairs={{0,2},{2,0},{4,6},{6,4},{8,10},{10,8},{12,14},{14,12},{16,18},{18,... | collective-permute-start | bytes 147464 | tf_op jit(solution)/shard_map/ppermute | solution.py:837
  211.1 4.2 %copy-start.4 = (bf16[16,64,1024]{2,1,0:T(8,128)(2,1)S(1)}, bf16[16,64,1024]{2,1,0:T(8,128)(2,1)}, u32[]{:S(2)}) copy-start(bf16[16,64,1024]{2,1,0:T(8,128)(2,1)} %get-tuple-element.112) | copy-start | bytes 6291460
  211.2 20.5 %collective-permute-start.30 = (bf16[16,64,1024]{2,1,0:T(8,128)(2,1)}, bf16[16,64,1024]{2,1,0:T(8,128)(2,1)S(1)}, u32[]{:S(2)}, u32[]{:S(2)}) collective-permute-start(bf16[16,64,1024]{2,1,0:T(8,128)(2,1)} %get-tuple-element.115), channel_id=1, source_target_pairs={{0,1},{1,0},{2,3},{3,2},{4,5},{5,4},{6,7},{7,6},{8,9},{9,8},{10,11... | collective-permute-start | bytes 6291464 | tf_op jit(solution)/shard_map/ppermute | solution.py:700
  213.3 4.2 %collective-permute-start.9 = (f32[96,128]{1,0:T(8,128)S(1)}, f32[96,128]{1,0:T(8,128)S(1)}, u32[]{:S(2)}, u32[]{:S(2)}) collective-permute-start(f32[96,128]{1,0:T(8,128)S(1)} %fusion.64), channel_id=1, source_target_pairs={{0,4},{2,6},{4,0},{6,2},{8,12},{10,14},{12,8},{14,10},{16,20},{18,... | collective-permute-start | bytes 147464 | tf_op jit(solution)/shard_map/ppermute | solution.py:837
  217.5 4.2 %collective-permute-start.10 = (f32[96,128]{1,0:T(8,128)S(1)}, f32[96,128]{1,0:T(8,128)S(1)}, u32[]{:S(2)}, u32[]{:S(2)}) collective-permute-start(f32[96,128]{1,0:T(8,128)S(1)} %add.587), channel_id=1, source_target_pairs={{0,8},{2,10},{4,12},{6,14},{8,0},{10,2},{12,4},{14,6},{16,24},{18,... | collective-permute-start | bytes 147464 | tf_op jit(solution)/shard_map/ppermute | solution.py:837
  219.9 5.2 %copy-start = (bf16[16,64,2048]{2,1,0:T(8,128)(2,1)S(1)}, bf16[16,64,2048]{2,1,0:T(8,128)(2,1)}, u32[]{:S(2)}) copy-start(bf16[16,64,2048]{2,1,0:T(8,128)(2,1)} %get-tuple-element.110) | copy-start | bytes 12582916
  221.6 5.6 %collective-permute-start.11 = (f32[96,128]{1,0:T(8,128)S(1)}, f32[96,128]{1,0:T(8,128)S(1)}, u32[]{:S(2)}, u32[]{:S(2)}) collective-permute-start(f32[96,128]{1,0:T(8,128)S(1)} %add.588), channel_id=1, source_target_pairs={{0,16},{2,18},{4,20},{6,22},{8,24},{10,26},{12,28},{14,30},{16,0},... | collective-permute-start | bytes 147464 | tf_op jit(solution)/shard_map/ppermute | solution.py:837
  227.3 112.4 %collective-permute-start.12 = (bf16[16,64,2048]{2,1,0:T(8,128)(2,1)S(1)}, bf16[16,64,2048]{2,1,0:T(8,128)(2,1)S(1)}, u32[]{:S(2)}, u32[]{:S(2)}) collective-permute-start(bf16[16,64,2048]{2,1,0:T(8,128)(2,1)S(1)} %copy-done.11), channel_id=1, source_target_pairs={{0,1},{1,0},{2,3},{3,2},{4,5},{5,4},{6,7},{7,6},{8,9},{9,8},{10,11... | collective-permute-start | bytes 12582920 | tf_op jit(solution)/shard_map/ppermute | solution.py:700
  234.3 30.5 %collective-permute-start.36 = (bf16[2,2,2,64,768]{4,3,1,0,2:T(8,128)(2,1)S(1)}, bf16[2,2,2,64,768]{4,3,1,0,2:T(8,128)(2,1)S(1)}, u32[]{:S(2)}, u32[]{:S(2)}) collective-permute-start(bf16[2,2,2,64,768]{4,3,1,0,2:T(8,128)(2,1)S(1)} %fusion.3), channel_id=1, source_target_pairs={{0,4},{2,6},{4,0},{6,2},{8,12},{10,14},{12,8},{14,10},{16,20},{18,... | collective-permute-start | bytes 2359304 | tf_op jit(solution)/shard_map/ppermute | solution.py:691
  237.8 14.8 %collective-permute-start.41 = (bf16[2,2,2,64,512]{4,3,2,1,0:T(8,128)(2,1)S(1)}, bf16[2,2,2,64,512]{4,3,2,1,0:T(8,128)(2,1)S(1)}, u32[]{:S(2)}, u32[]{:S(2)}) collective-permute-start(bf16[2,2,2,64,512]{4,3,2,1,0:T(8,128)(2,1)S(1)} %fusion.8), channel_id=1, source_target_pairs={{0,8},{2,10},{4,12},{6,14},{8,0},{10,2},{12,4},{14,6},{16,24},{18,... | collective-permute-start | bytes 1572872 | tf_op jit(solution)/shard_map/ppermute | solution.py:691
  239.4 39.6 %collective-permute-start.49 = (bf16[2,2,2,64,768]{4,3,1,0,2:T(8,128)(2,1)S(1)}, bf16[2,2,2,64,768]{4,3,1,0,2:T(8,128)(2,1)S(1)}, u32[]{:S(2)}, u32[]{:S(2)}) collective-permute-start(bf16[2,2,2,64,768]{4,3,1,0,2:T(8,128)(2,1)S(1)} %fusion.5), channel_id=1, source_target_pairs={{0,2},{2,0},{4,6},{6,4},{8,10},{10,8},{12,14},{14,12},{16,18},{18,... | collective-permute-start | bytes 2359304 | tf_op jit(solution)/shard_map/ppermute | solution.py:691
  242.0 21.1 %collective-permute-start.31 = (bf16[2,2,2,64,512]{4,3,2,1,0:T(8,128)(2,1)S(1)}, bf16[2,2,2,64,512]{4,3,2,1,0:T(8,128)(2,1)S(1)}, u32[]{:S(2)}, u32[]{:S(2)}) collective-permute-start(bf16[2,2,2,64,512]{4,3,2,1,0:T(8,128)(2,1)S(1)} %fusion.7), channel_id=1, source_target_pairs={{0,8},{2,10},{4,12},{6,14},{8,0},{10,2},{12,4},{14,6},{16,24},{18,... | collective-permute-start | bytes 1572872 | tf_op jit(solution)/shard_map/ppermute | solution.py:691
  252.6 40.8 %collective-permute-start.26 = (bf16[2,2,2,64,768]{4,3,1,0,2:T(8,128)(2,1)S(1)}, bf16[2,2,2,64,768]{4,3,1,0,2:T(8,128)(2,1)S(1)}, u32[]{:S(2)}, u32[]{:S(2)}) collective-permute-start(bf16[2,2,2,64,768]{4,3,1,0,2:T(8,128)(2,1)S(1)} %fusion.2), channel_id=1, source_target_pairs={{0,4},{2,6},{4,0},{6,2},{8,12},{10,14},{12,8},{14,10},{16,20},{18,... | collective-permute-start | bytes 2359304 | tf_op jit(solution)/shard_map/ppermute | solution.py:691
  263.1 31.1 %collective-permute-start.45 = (bf16[2,2,2,64,768]{4,3,1,0,2:T(8,128)(2,1)S(1)}, bf16[2,2,2,64,768]{4,3,1,0,2:T(8,128)(2,1)S(1)}, u32[]{:S(2)}, u32[]{:S(2)}) collective-permute-start(bf16[2,2,2,64,768]{4,3,1,0,2:T(8,128)(2,1)S(1)} %fusion.4), channel_id=1, source_target_pairs={{0,2},{2,0},{4,6},{6,4},{8,10},{10,8},{12,14},{14,12},{16,18},{18,... | collective-permute-start | bytes 2359304 | tf_op jit(solution)/shard_map/ppermute | solution.py:691
  264.8 14.2 %collective-permute-start.42 = (bf16[2,2,64,512]{3,2,1,0:T(8,128)(2,1)S(1)}, bf16[2,2,64,512]{3,2,1,0:T(8,128)(2,1)S(1)}, u32[]{:S(2)}, u32[]{:S(2)}) collective-permute-start(bf16[2,2,64,512]{3,2,1,0:T(8,128)(2,1)S(1)} %fusion.9), channel_id=1, source_target_pairs={{0,16},{2,18},{4,20},{6,22},{8,24},{10,26},{12,28},{14,30},{16,0},... | collective-permute-start | bytes 786440 | tf_op jit(solution)/shard_map/ppermute | solution.py:691
  279.0 13.7 %collective-permute-start.32 = (bf16[2,2,64,512]{3,2,1,0:T(8,128)(2,1)S(1)}, bf16[2,2,64,512]{3,2,1,0:T(8,128)(2,1)S(1)}, u32[]{:S(2)}, u32[]{:S(2)}) collective-permute-start(bf16[2,2,64,512]{3,2,1,0:T(8,128)(2,1)S(1)} %fusion.10), channel_id=1, source_target_pairs={{0,16},{2,18},{4,20},{6,22},{8,24},{10,26},{12,28},{14,30},{16,0},... | collective-permute-start | bytes 786440 | tf_op jit(solution)/shard_map/ppermute | solution.py:691
  279.0 32.7 %collective-permute-start.37 = (bf16[2,2,64,768]{3,2,1,0:T(8,128)(2,1)S(1)}, bf16[2,2,64,768]{3,2,1,0:T(8,128)(2,1)S(1)}, u32[]{:S(2)}, u32[]{:S(2)}) collective-permute-start(bf16[2,2,64,768]{3,2,1,0:T(8,128)(2,1)S(1)} %fusion.15), channel_id=1, source_target_pairs={{0,2},{2,0},{4,6},{6,4},{8,10},{10,8},{12,14},{14,12},{16,18},{18,... | collective-permute-start | bytes 1179656 | tf_op jit(solution)/shard_map/ppermute | solution.py:691
  292.7 5.4 %collective-permute-start.43 = (bf16[2,64,512]{2,1,0:T(8,128)(2,1)S(1)}, bf16[2,64,512]{2,1,0:T(8,128)(2,1)S(1)}, u32[]{:S(2)}, u32[]{:S(2)}) collective-permute-start(bf16[2,64,512]{2,1,0:T(8,128)(2,1)S(1)} %fusion.38), channel_id=1, source_target_pairs={{0,2},{2,0},{4,6},{6,4},{8,10},{10,8},{12,14},{14,12},{16,18},{18,... | collective-permute-start | bytes 393224 | tf_op jit(solution)/shard_map/ppermute | solution.py:691
  293.4 18.5 %collective-permute-start.50 = (bf16[2,2,64,768]{3,2,1,0:T(8,128)(2,1)S(1)}, bf16[2,2,64,768]{3,2,1,0:T(8,128)(2,1)S(1)}, u32[]{:S(2)}, u32[]{:S(2)}) collective-permute-start(bf16[2,2,64,768]{3,2,1,0:T(8,128)(2,1)S(1)} %fusion.17), channel_id=1, source_target_pairs={{0,4},{2,6},{4,0},{6,2},{8,12},{10,14},{12,8},{14,10},{16,20},{18,... | collective-permute-start | bytes 1179656 | tf_op jit(solution)/shard_map/ppermute | solution.py:691
  294.2 6.7 %collective-permute-start.33 = (bf16[2,64,512]{2,1,0:T(8,128)(2,1)S(1)}, bf16[2,64,512]{2,1,0:T(8,128)(2,1)S(1)}, u32[]{:S(2)}, u32[]{:S(2)}) collective-permute-start(bf16[2,64,512]{2,1,0:T(8,128)(2,1)S(1)} %fusion.37), channel_id=1, source_target_pairs={{0,2},{2,0},{4,6},{6,4},{8,10},{10,8},{12,14},{14,12},{16,18},{18,... | collective-permute-start | bytes 393224 | tf_op jit(solution)/shard_map/ppermute | solution.py:691
  298.1 16.0 %collective-permute-start.27 = (bf16[2,2,64,768]{3,2,1,0:T(8,128)(2,1)S(1)}, bf16[2,2,64,768]{3,2,1,0:T(8,128)(2,1)S(1)}, u32[]{:S(2)}, u32[]{:S(2)}) collective-permute-start(bf16[2,2,64,768]{3,2,1,0:T(8,128)(2,1)S(1)} %fusion.14), channel_id=1, source_target_pairs={{0,2},{2,0},{4,6},{6,4},{8,10},{10,8},{12,14},{14,12},{16,18},{18,... | collective-permute-start | bytes 1179656 | tf_op jit(solution)/shard_map/ppermute | solution.py:691
  300.9 4.3 %collective-permute-start.44 = (bf16[64,512]{1,0:T(8,128)(2,1)S(1)}, bf16[64,512]{1,0:T(8,128)(2,1)S(1)}, u32[]{:S(2)}, u32[]{:S(2)}) collective-permute-start(bf16[64,512]{1,0:T(8,128)(2,1)S(1)} %fusion.39), channel_id=1, source_target_pairs={{0,4},{2,6},{4,0},{6,2},{8,12},{10,14},{12,8},{14,10},{16,20},{18,... | collective-permute-start | bytes 196616 | tf_op jit(solution)/shard_map/ppermute | solution.py:691
  305.2 5.0 %collective-permute-start.34 = (bf16[64,512]{1,0:T(8,128)(2,1)S(1)}, bf16[64,512]{1,0:T(8,128)(2,1)S(1)}, u32[]{:S(2)}, u32[]{:S(2)}) collective-permute-start(bf16[64,512]{1,0:T(8,128)(2,1)S(1)} %fusion.41), channel_id=1, source_target_pairs={{0,4},{2,6},{4,0},{6,2},{8,12},{10,14},{12,8},{14,10},{16,20},{18,... | collective-permute-start | bytes 196616 | tf_op jit(solution)/shard_map/ppermute | solution.py:691
  310.2 7.8 %collective-permute-start.46 = (bf16[2,2,64,768]{3,2,1,0:T(8,128)(2,1)S(1)}, bf16[2,2,64,768]{3,2,1,0:T(8,128)(2,1)S(1)}, u32[]{:S(2)}, u32[]{:S(2)}) collective-permute-start(bf16[2,2,64,768]{3,2,1,0:T(8,128)(2,1)S(1)} %fusion.16), channel_id=1, source_target_pairs={{0,4},{2,6},{4,0},{6,2},{8,12},{10,14},{12,8},{14,10},{16,20},{18,... | collective-permute-start | bytes 1179656 | tf_op jit(solution)/shard_map/ppermute | solution.py:691
  311.9 8.8 %collective-permute-start.38 = (bf16[2,64,768]{2,1,0:T(8,128)(2,1)S(1)}, bf16[2,64,768]{2,1,0:T(8,128)(2,1)S(1)}, u32[]{:S(2)}, u32[]{:S(2)}) collective-permute-start(bf16[2,64,768]{2,1,0:T(8,128)(2,1)S(1)} %fusion.21), channel_id=1, source_target_pairs={{0,8},{2,10},{4,12},{6,14},{8,0},{10,2},{12,4},{14,6},{16,24},{18,... | collective-permute-start | bytes 589832 | tf_op jit(solution)/shard_map/ppermute | solution.py:691
  312.1 12.9 %collective-permute-start.51 = (bf16[2,64,768]{2,1,0:T(8,128)(2,1)S(1)}, bf16[2,64,768]{2,1,0:T(8,128)(2,1)S(1)}, u32[]{:S(2)}, u32[]{:S(2)}) collective-permute-start(bf16[2,64,768]{2,1,0:T(8,128)(2,1)S(1)} %fusion.23), channel_id=1, source_target_pairs={{0,8},{2,10},{4,12},{6,14},{8,0},{10,2},{12,4},{14,6},{16,24},{18,... | collective-permute-start | bytes 589832 | tf_op jit(solution)/shard_map/ppermute | solution.py:691
  314.3 13.9 %collective-permute-start.28 = (bf16[2,64,768]{2,1,0:T(8,128)(2,1)S(1)}, bf16[2,64,768]{2,1,0:T(8,128)(2,1)S(1)}, u32[]{:S(2)}, u32[]{:S(2)}) collective-permute-start(bf16[2,64,768]{2,1,0:T(8,128)(2,1)S(1)} %fusion.20), channel_id=1, source_target_pairs={{0,8},{2,10},{4,12},{6,14},{8,0},{10,2},{12,4},{14,6},{16,24},{18,... | collective-permute-start | bytes 589832 | tf_op jit(solution)/shard_map/ppermute | solution.py:691
  318.1 13.5 %collective-permute-start.47 = (bf16[2,64,768]{2,1,0:T(8,128)(2,1)S(1)}, bf16[2,64,768]{2,1,0:T(8,128)(2,1)S(1)}, u32[]{:S(2)}, u32[]{:S(2)}) collective-permute-start(bf16[2,64,768]{2,1,0:T(8,128)(2,1)S(1)} %fusion.22), channel_id=1, source_target_pairs={{0,8},{2,10},{4,12},{6,14},{8,0},{10,2},{12,4},{14,6},{16,24},{18,... | collective-permute-start | bytes 589832 | tf_op jit(solution)/shard_map/ppermute | solution.py:691
  320.7 11.0 %collective-permute-start.39 = (bf16[64,768]{1,0:T(8,128)(2,1)S(1)}, bf16[64,768]{1,0:T(8,128)(2,1)S(1)}, u32[]{:S(2)}, u32[]{:S(2)}) collective-permute-start(bf16[64,768]{1,0:T(8,128)(2,1)S(1)} %fusion.28), channel_id=1, source_target_pairs={{0,16},{2,18},{4,20},{6,22},{8,24},{10,26},{12,28},{14,30},{16,0},... | collective-permute-start | bytes 294920 | tf_op jit(solution)/shard_map/ppermute | solution.py:691
  325.1 10.5 %collective-permute-start.52 = (bf16[64,768]{1,0:T(8,128)(2,1)S(1)}, bf16[64,768]{1,0:T(8,128)(2,1)S(1)}, u32[]{:S(2)}, u32[]{:S(2)}) collective-permute-start(bf16[64,768]{1,0:T(8,128)(2,1)S(1)} %fusion.24), channel_id=1, source_target_pairs={{0,16},{2,18},{4,20},{6,22},{8,24},{10,26},{12,28},{14,30},{16,0},... | collective-permute-start | bytes 294920 | tf_op jit(solution)/shard_map/ppermute | solution.py:691
  328.2 9.5 %collective-permute-start.29 = (bf16[64,768]{1,0:T(8,128)(2,1)S(1)}, bf16[64,768]{1,0:T(8,128)(2,1)S(1)}, u32[]{:S(2)}, u32[]{:S(2)}) collective-permute-start(bf16[64,768]{1,0:T(8,128)(2,1)S(1)} %fusion.30), channel_id=1, source_target_pairs={{0,16},{2,18},{4,20},{6,22},{8,24},{10,26},{12,28},{14,30},{16,0},... | collective-permute-start | bytes 294920 | tf_op jit(solution)/shard_map/ppermute | solution.py:691
  331.7 7.1 %collective-permute-start.48 = (bf16[64,768]{1,0:T(8,128)(2,1)S(1)}, bf16[64,768]{1,0:T(8,128)(2,1)S(1)}, u32[]{:S(2)}, u32[]{:S(2)}) collective-permute-start(bf16[64,768]{1,0:T(8,128)(2,1)S(1)} %fusion.26), channel_id=1, source_target_pairs={{0,16},{2,18},{4,20},{6,22},{8,24},{10,26},{12,28},{14,30},{16,0},... | collective-permute-start | bytes 294920 | tf_op jit(solution)/shard_map/ppermute | solution.py:691
  341.1 10.5 %collective-permute-start.21 = (bf16[2,2,2,64,512]{4,3,2,1,0:T(8,128)(2,1)S(1)}, bf16[2,2,2,64,512]{4,3,2,1,0:T(8,128)(2,1)S(1)}, u32[]{:S(2)}, u32[]{:S(2)}) collective-permute-start(bf16[2,2,2,64,512]{4,3,2,1,0:T(8,128)(2,1)S(1)} %fusion.6), channel_id=1, source_target_pairs={{0,8},{2,10},{4,12},{6,14},{8,0},{10,2},{12,4},{14,6},{16,24},{18,... | collective-permute-start | bytes 1572872 | tf_op jit(solution)/shard_map/ppermute | solution.py:691
  341.5 23.9 %collective-permute-start.13 = (bf16[2,2,2,64,768]{4,3,1,0,2:T(8,128)(2,1)S(1)}, bf16[2,2,2,64,768]{4,3,1,0,2:T(8,128)(2,1)S(1)}, u32[]{:S(2)}, u32[]{:S(2)}) collective-permute-start(bf16[2,2,2,64,768]{4,3,1,0,2:T(8,128)(2,1)S(1)} %fusion), channel_id=1, source_target_pairs={{0,2},{2,0},{4,6},{6,4},{8,10},{10,8},{12,14},{14,12},{16,18},{18,... | collective-permute-start | bytes 2359304 | tf_op jit(solution)/shard_map/ppermute | solution.py:691
  343.2 23.8 %collective-permute-start.17 = (bf16[2,2,2,64,768]{4,3,1,0,2:T(8,128)(2,1)S(1)}, bf16[2,2,2,64,768]{4,3,1,0,2:T(8,128)(2,1)S(1)}, u32[]{:S(2)}, u32[]{:S(2)}) collective-permute-start(bf16[2,2,2,64,768]{4,3,1,0,2:T(8,128)(2,1)S(1)} %fusion.1), channel_id=1, source_target_pairs={{0,4},{2,6},{4,0},{6,2},{8,12},{10,14},{12,8},{14,10},{16,20},{18,... | collective-permute-start | bytes 2359304 | tf_op jit(solution)/shard_map/ppermute | solution.py:691
  351.7 12.3 %collective-permute-start.22 = (bf16[2,2,64,512]{3,2,1,0:T(8,128)(2,1)S(1)}, bf16[2,2,64,512]{3,2,1,0:T(8,128)(2,1)S(1)}, u32[]{:S(2)}, u32[]{:S(2)}) collective-permute-start(bf16[2,2,64,512]{3,2,1,0:T(8,128)(2,1)S(1)} %fusion.11), channel_id=1, source_target_pairs={{0,16},{2,18},{4,20},{6,22},{8,24},{10,26},{12,28},{14,30},{16,0},... | collective-permute-start | bytes 786440 | tf_op jit(solution)/shard_map/ppermute | solution.py:691
  364.0 6.2 %collective-permute-start.23 = (bf16[2,64,512]{2,1,0:T(8,128)(2,1)S(1)}, bf16[2,64,512]{2,1,0:T(8,128)(2,1)S(1)}, u32[]{:S(2)}, u32[]{:S(2)}) collective-permute-start(bf16[2,64,512]{2,1,0:T(8,128)(2,1)S(1)} %fusion.36), channel_id=1, source_target_pairs={{0,2},{2,0},{4,6},{6,4},{8,10},{10,8},{12,14},{14,12},{16,18},{18,... | collective-permute-start | bytes 393224 | tf_op jit(solution)/shard_map/ppermute | solution.py:691
  365.5 11.9 %collective-permute-start.14 = (bf16[2,2,64,768]{3,2,1,0:T(8,128)(2,1)S(1)}, bf16[2,2,64,768]{3,2,1,0:T(8,128)(2,1)S(1)}, u32[]{:S(2)}, u32[]{:S(2)}) collective-permute-start(bf16[2,2,64,768]{3,2,1,0:T(8,128)(2,1)S(1)} %fusion.12), channel_id=1, source_target_pairs={{0,4},{2,6},{4,0},{6,2},{8,12},{10,14},{12,8},{14,10},{16,20},{18,... | collective-permute-start | bytes 1179656 | tf_op jit(solution)/shard_map/ppermute | solution.py:691
  367.1 11.4 %collective-permute-start.18 = (bf16[2,2,64,768]{3,2,1,0:T(8,128)(2,1)S(1)}, bf16[2,2,64,768]{3,2,1,0:T(8,128)(2,1)S(1)}, u32[]{:S(2)}, u32[]{:S(2)}) collective-permute-start(bf16[2,2,64,768]{3,2,1,0:T(8,128)(2,1)S(1)} %fusion.13), channel_id=1, source_target_pairs={{0,2},{2,0},{4,6},{6,4},{8,10},{10,8},{12,14},{14,12},{16,18},{18,... | collective-permute-start | bytes 1179656 | tf_op jit(solution)/shard_map/ppermute | solution.py:691
  370.2 6.5 %collective-permute-start.24 = (bf16[64,512]{1,0:T(8,128)(2,1)S(1)}, bf16[64,512]{1,0:T(8,128)(2,1)S(1)}, u32[]{:S(2)}, u32[]{:S(2)}) collective-permute-start(bf16[64,512]{1,0:T(8,128)(2,1)S(1)} %fusion.43), channel_id=1, source_target_pairs={{0,4},{2,6},{4,0},{6,2},{8,12},{10,14},{12,8},{14,10},{16,20},{18,... | collective-permute-start | bytes 196616 | tf_op jit(solution)/shard_map/ppermute | solution.py:691
  377.6 7.8 %collective-permute-start.15 = (bf16[2,64,768]{2,1,0:T(8,128)(2,1)S(1)}, bf16[2,64,768]{2,1,0:T(8,128)(2,1)S(1)}, u32[]{:S(2)}, u32[]{:S(2)}) collective-permute-start(bf16[2,64,768]{2,1,0:T(8,128)(2,1)S(1)} %fusion.18), channel_id=1, source_target_pairs={{0,8},{2,10},{4,12},{6,14},{8,0},{10,2},{12,4},{14,6},{16,24},{18,... | collective-permute-start | bytes 589832 | tf_op jit(solution)/shard_map/ppermute | solution.py:691
  378.7 9.2 %collective-permute-start.19 = (bf16[2,64,768]{2,1,0:T(8,128)(2,1)S(1)}, bf16[2,64,768]{2,1,0:T(8,128)(2,1)S(1)}, u32[]{:S(2)}, u32[]{:S(2)}) collective-permute-start(bf16[2,64,768]{2,1,0:T(8,128)(2,1)S(1)} %fusion.19), channel_id=1, source_target_pairs={{0,8},{2,10},{4,12},{6,14},{8,0},{10,2},{12,4},{14,6},{16,24},{18,... | collective-permute-start | bytes 589832 | tf_op jit(solution)/shard_map/ppermute | solution.py:691
  385.5 7.0 %collective-permute-start.16 = (bf16[64,768]{1,0:T(8,128)(2,1)S(1)}, bf16[64,768]{1,0:T(8,128)(2,1)S(1)}, u32[]{:S(2)}, u32[]{:S(2)}) collective-permute-start(bf16[64,768]{1,0:T(8,128)(2,1)S(1)} %fusion.34), channel_id=1, source_target_pairs={{0,16},{2,18},{4,20},{6,22},{8,24},{10,26},{12,28},{14,30},{16,0},... | collective-permute-start | bytes 294920 | tf_op jit(solution)/shard_map/ppermute | solution.py:691
  388.0 7.2 %collective-permute-start.20 = (bf16[64,768]{1,0:T(8,128)(2,1)S(1)}, bf16[64,768]{1,0:T(8,128)(2,1)S(1)}, u32[]{:S(2)}, u32[]{:S(2)}) collective-permute-start(bf16[64,768]{1,0:T(8,128)(2,1)S(1)} %fusion.32), channel_id=1, source_target_pairs={{0,16},{2,18},{4,20},{6,22},{8,24},{10,26},{12,28},{14,30},{16,0},... | collective-permute-start | bytes 294920 | tf_op jit(solution)/shard_map/ppermute | solution.py:691
  (4 other events, 6.6 us)
